TPU v7x, 512 devices: a whole 4x4x16 slice. The times are simulated.
512 devices in a mesh: wide: 128 (over y, z, x_lo), mp: 4 (over x_hi, core).
Axes of the slice: x: 4 (x_hi: 2, x_lo: 2; x = x_hi * 2 + x_lo), y: 4, z: 16, core: 2. Of those that a mesh axis runs over, the one named last changes fastest.
Arguments:
- clip_feats: bfloat16 [16384, 768], P('wide'), may hold values from -6 to 6
- teacher_audio: bfloat16 [16384, 512], P('wide'), may hold values from -16 to 16
- teacher_text: bfloat16 [16384, 512], P(('wide', 'mp')), may hold values from -16 to 16
- w_first: bfloat16 [768, 512], P(None, 'mp'), may hold values from -0.21875 to 0.21875
- w_second: bfloat16 [512, 512], P('mp'), may hold values from -0.25 to 0.25
- pairing: int32 [16384], P('wide'), may hold values from 0 to 16383
Outputs:
- loss: float32 [], replicated
- grad_first: float32 [768, 512], P(None, 'mp')
- grad_second: float32 [512, 512], P('mp')
All inputs are finite; a program needn't handle non-finite values.
Results may differ from a plain program's by a relative error of at most 0.0052.
Values may be sent and summed in bfloat16 or wider, within the bound.
A program may use at most 64 MiB of HBM per device.

v0:
```python
import math

import jax
import jax.numpy as jnp
from jax import lax
from jax.sharding import Mesh
from jax.sharding import PartitionSpec as P

WIDE = ("wide_0", "wide_1", "wide_2")
WIDE_MP = ("wide_0", "wide_1", "wide_2", "mp")


teacher_scale = 14.0
student_scale = 64.0
eps = 1e-06


def from_everyone(array, axis):
    devices = lax.axis_size(axis)
    return lax.all_to_all(
        jnp.broadcast_to(array[None], (devices, *array.shape)), axis, 0, 0, tiled=True
    )


def taken_together(array, axis):
    return from_everyone(array, axis).sum(axis=0)


def in_order(parts, dim):
    dims = list(parts.shape[1:])
    dims[dim] *= parts.shape[0]
    return jnp.moveaxis(parts, 0, dim).reshape(dims)


def all_blocks(array, axes, order):
    parts = array
    for k in order:
        parts = lax.all_gather(parts, axes[k])
    done = order[::-1]
    back = [done.index(k) for k in range(len(axes))]
    parts = parts.transpose(*back, *range(len(axes), parts.ndim))
    return parts.reshape(-1, *array.shape)


def gathered_by_axis(array, axes, order, dim):
    return in_order(all_blocks(array, axes, order), dim)


def filled_up(lines, devices):
    spare = -len(lines) % devices
    return jnp.pad(lines, [(0, spare)] + [(0, 0)] * (lines.ndim - 1))


def whole_of(array, axes, dim):
    far, near = axes
    parts = from_everyone(from_everyone(array, far), near)
    return in_order(parts.swapaxes(0, 1).reshape(-1, *array.shape), dim)


def split_up(array, dim, devices):
    dims = array.shape
    parts = array.reshape(*dims[:dim], devices, dims[dim] // devices, *dims[dim + 1 :])
    return jnp.moveaxis(parts, dim, 0)


def summed_on_arrival(array, axis, dim):
    devices = lax.axis_size(axis)
    parts = lax.all_to_all(split_up(array, dim, devices), axis, 0, 0, tiled=True)
    return jnp.sum(parts, axis=0)


def summed_rows(array, axes, dim):
    far, near = axes
    parts = split_up(array, dim, lax.axis_size(far))
    nearer = summed_on_arrival(parts, near, dim + 1)
    arrived = lax.all_to_all(nearer, far, split_axis=0, concat_axis=0, tiled=True)
    return arrived.sum(axis=0)


def total_of(array, axes):
    padded = filled_up(array, lax.axis_size(axes[0]) * lax.axis_size(axes[1]))
    whole = whole_of(summed_rows(padded, axes, 0), axes, 0)
    return lax.slice_in_dim(whole, 0, len(array)).reshape(array.shape)


def in_one(arrays, axis):
    ends = [0]
    for a in arrays:
        ends.append(ends[-1] + a.size)
    total = total_of(jnp.concatenate([a.ravel() for a in arrays]), axis)
    return tuple((total[b:e].reshape(a.shape) for a, b, e in zip(arrays, ends, ends[1:])))


def normalize(values):
    return values / jnp.sqrt(jnp.sum(values * values, axis=1, keepdims=True) + eps)


def inner_rows(left, right):
    return lax.dot_general(
        left, right, (((1,), (1,)), ((), ())), preferred_element_type=jnp.float32
    )


def sweep(work, initial, source, base):
    count = source.shape[0]
    width = math.gcd(count, 2048)
    block_count = count // width

    def advance(index, carry):
        block = lax.dynamic_slice_in_dim(source, index * width, width, 0)
        return work(carry, block, base + index * width)

    return lax.fori_loop(0, block_count, advance, initial)


def body(clip_feats, teacher_audio, teacher_text, w_first, w_second, pairing):
    row_count = clip_feats.shape[0]
    total = row_count * lax.axis_size(WIDE)
    quarter = teacher_text.shape[0]
    mp_size = lax.axis_size("mp")
    mp_index = lax.axis_index("mp")
    pre_act = jnp.dot(clip_feats, w_first, preferred_element_type=jnp.float32)
    gelu_out, gelu_back = jax.vjp(lambda u: jax.nn.gelu(u, approximate=False), pre_act)
    hidden = gelu_out.astype(jnp.bfloat16)
    raw = taken_together(jnp.dot(hidden, w_second, preferred_element_type=jnp.float32), "mp")
    norm = jnp.sqrt(jnp.sum(raw * raw, axis=1, keepdims=True) + eps)
    student = raw / norm
    stacked = jnp.concatenate(
        [
            normalize(teacher_audio.astype(jnp.float32)).astype(jnp.bfloat16),
            student.astype(jnp.bfloat16),
        ],
        axis=0,
    )
    capt_local = normalize(teacher_text.astype(jnp.float32)).astype(jnp.bfloat16)

    def logits(block, start):
        scores = inner_rows(stacked, block)
        local_ids = start + jnp.arange(block.shape[0], dtype=jnp.int32)
        global_ids = (
            local_ids // quarter * (quarter * mp_size) + mp_index * quarter + local_ids % quarter
        )
        hit = global_ids[None, :] == pairing[:, None]
        return (teacher_scale * scores[:row_count], student_scale * scores[row_count:], hit)

    def first_pass(carry, block, start):
        tlog, slog, hit = logits(block, start)
        texp = jnp.exp(tlog)
        sexp = jnp.exp(slog)
        return (
            carry[0] + jnp.sum(texp, axis=1),
            carry[1] + jnp.sum(sexp, axis=1),
            carry[2] + jnp.sum(texp * (tlog - slog), axis=1),
            carry[3] + jnp.sum(jnp.where(hit, slog, 0.0), axis=1),
        )

    zeros_row = jnp.zeros((row_count,), jnp.float32)
    first_init = (zeros_row, zeros_row, zeros_row, zeros_row)
    zeros_grad = jnp.zeros((row_count, stacked.shape[1]), jnp.float32)

    def make_second(zt_sum, zs_sum):

        def second_pass(carry, block, start):
            tlog, slog, hit = logits(block, start)
            coef = (
                2.0 * jnp.exp(slog) / zs_sum[:, None]
                - jnp.exp(tlog) / zt_sum[:, None]
                - hit.astype(jnp.float32)
            ).astype(jnp.bfloat16)
            return carry + jnp.dot(coef, block, preferred_element_type=jnp.float32)

        return second_pass

    gathered = gathered_by_axis(capt_local, WIDE, (2, 0, 1), 0)
    partial_stats = sweep(first_pass, first_init, gathered, 0)
    zt_sum, zs_sum, acc_sum, spair = jax.tree.map(
        lambda part: taken_together(part, "mp"), partial_stats
    )
    second_pass = make_second(zt_sum, zs_sum)
    dpart = sweep(second_pass, zeros_grad, gathered, 0)
    loss_part = jnp.sum(acc_sum / zt_sum - jnp.log(zt_sum) + 2.0 * jnp.log(zs_sum) - spair)
    dstud = taken_together(dpart, "mp") * (student_scale / total)
    draw = ((dstud - student * jnp.sum(student * dstud, axis=1, keepdims=True)) / norm).astype(
        jnp.bfloat16
    )
    grad_second = jnp.dot(hidden.T, draw, preferred_element_type=jnp.float32)
    dhid = lax.dot_general(
        draw, w_second, (((1,), (1,)), ((), ())), preferred_element_type=jnp.float32
    )
    dpre = gelu_back(dhid)[0].astype(jnp.bfloat16)
    grad_first = jnp.dot(clip_feats.T, dpre, preferred_element_type=jnp.float32)
    grad_first, grad_second, loss_sum = in_one(
        (grad_first, grad_second, loss_part), (("wide_0", "wide_1"), "wide_2")
    )
    return (loss_sum / total, grad_first, grad_second)


def solution(mesh):
    finer = Mesh(
        mesh.devices.reshape(4, 16, 2, mesh.shape["mp"]), ("wide_0", "wide_1", "wide_2", "mp")
    )
    return jax.shard_map(
        body,
        mesh=finer,
        in_specs=(
            P(WIDE, None),
            P(WIDE, None),
            P(WIDE_MP, None),
            P(None, "mp"),
            P("mp", None),
            P(WIDE),
        ),
        out_specs=(P(), P(None, "mp"), P("mp", None)),
        check_vma=False,
    )
```

profile of v0, /device:TPU:24, one launch (start us, length us, event | category | flops | bytes accessed | tf_op | source)
XLA Modules:
  0.0 285.4 jit_solution(2616207813404230353)
XLA Ops:
  7.2 1.0 fusion.51
  8.2 0.8 fusion.52
  9.1 4.6 %all-gather = bf16[64,512]{1,0:T(8,128)(2,1)S(1)} all-gather(bf16[32,512]{1,0:T(8,128)(2,1)S(1)} %fusion.52), channel_id=2, replica_groups=mesh['wide_0'=4,'wide_1'=16,'wide_2'=2,'mp'=4] {'wide_2'}, dimensions={0}, use_global_device_ids=true | all-gather | bytes 98304 | tf_op jit(solution)/shard_map/all_gather | solution.py:38
  13.6 15.4 %all-gather.1 = bf16[8,32,512]{2,1,0:T(8,128)(2,1)} all-gather(bf16[2,32,512]{2,1,0:T(8,128)(2,1)S(1)} %bitcast.54), channel_id=3, replica_groups=mesh['wide_0'=4,'wide_1'=16,'wide_2'=2,'mp'=4] {'wide_0'}, dimensions={0}, use_global_device_ids=true | all-gather | bytes 327680 | tf_op jit(solution)/shard_map/all_gather | solution.py:38
  29.0 1.3 multiply_convert_fusion
  30.5 1.1 broadcast_in_dim.90
  31.6 3.5 %all-to-all-start = ((f32[4,128,512]{2,1,0:T(8,128)}), f32[4,128,512]{2,1,0:T(8,128)S(1)}, u32[]{:S(2)}, u32[]{:S(2)}) async-start(f32[4,128,512]{2,1,0:T(8,128)} %broadcast_in_dim.90), calls=%async_computation | async-start | bytes 2097152 | tf_op jit(solution)/shard_map/all_to_all | solution.py:20
  35.4 15.6 %all-to-all-done = f32[4,128,512]{2,1,0:T(8,128)S(1)} async-done(((f32[4,128,512]{2,1,0:T(8,128)}), f32[4,128,512]{2,1,0:T(8,128)S(1)}, u32[]{:S(2)}, u32[]{:S(2)}) %all-to-all-start) | async-done | bytes 1048608 | tf_op jit(solution)/shard_map/all_to_all | solution.py:20
  51.4 58.2 %all-gather.5.cloned.1.call-done = bf16[64,2,32,512]{3,2,1,0:T(8,128)(2,1)} async-done(((bf16[4,2,32,512]{3,2,1,0:T(8,128)(2,1)}), bf16[64,2,32,512]{3,2,1,0:T(8,128)(2,1)}) %all-gather.5.cloned.1.call-update) | async-done | bytes 4194320 | tf_op jit(solution)/shard_map/all_gather | solution.py:38
  109.6 4.8 %copy.24 = bf16[4,16,2,32,512]{4,3,2,1,0:T(8,128)(2,1)} copy(bf16[4,16,2,32,512]{4,3,2,0,1:T(8,128)(2,1)} %bitcast.47) | data formatting | bytes 8388608 | tf_op jit(solution)/shard_map/transpose | solution.py:41
  114.3 5.9 %while.38 = (s32[]{:T(128)}, f32[128]{0:T(128)S(1)}, f32[128]{0:T(128)S(1)}, f32[128]{0:T(128)S(1)}, f32[128]{0:T(128)S(1)}, /*index=5*/bf16[4096,512]{1,0:T(8,1...) while((s32[]{:T(128)}, f32[128]{0:T(128)S(1)}, ...), condition=%wide.region_9.10_spmd.clone, body=%wide.region_4.9_spmd.clone.sunk | while | flops 539539968 | bytes 6578890 | solution.py:113
  114.3 2.3 convolution_bitcast_fusion.6
  116.7 0.6 select_reduce_fusion.2
  117.3 2.3 convolution_bitcast_fusion.6
  119.7 0.6 select_reduce_fusion.2
  120.3 9.4 %all_to_all.59 = f32[4,1,128]{2,1,0:T(1,128)S(1)} all-to-all(f32[4,1,128]{2,1,0:T(1,128)S(1)} %broadcast_in_dim.92), channel_id=1, replica_groups=mesh['wide_0'=4,'wide_1'=16,'wide_2'=2,'mp'=4] {'mp'}, dimensions={0} | all-to-all | bytes 4096 | tf_op jit(solution)/shard_map/all_to_all | solution.py:20
  129.7 7.6 %all_to_all.60 = f32[4,1,128]{2,1,0:T(1,128)S(1)} all-to-all(f32[4,1,128]{2,1,0:T(1,128)S(1)} %broadcast_in_dim.93), channel_id=1, replica_groups=mesh['wide_0'=4,'wide_1'=16,'wide_2'=2,'mp'=4] {'mp'}, dimensions={0} | all-to-all | bytes 4096 | tf_op jit(solution)/shard_map/all_to_all | solution.py:20
  137.2 0.6 broadcast_in_dim.96
  137.8 3.2 %all-to-all-start.5 = ((f32[4,1,128]{2,1,0:T(1,128)}), f32[4,1,128]{2,1,0:T(1,128)S(1)}, u32[]{:S(2)}, u32[]{:S(2)}) async-start(f32[4,1,128]{2,1,0:T(1,128)} %broadcast_in_dim.96), calls=%async_computation.5 | async-start | bytes 4096 | tf_op jit(solution)/shard_map/all_to_all | solution.py:20
  141.1 5.1 %all-to-all-done.5 = f32[4,1,128]{2,1,0:T(1,128)S(1)} async-done(((f32[4,1,128]{2,1,0:T(1,128)}), f32[4,1,128]{2,1,0:T(1,128)S(1)}, u32[]{:S(2)}, u32[]{:S(2)}) %all-to-all-start.5) | async-done | bytes 2080 | tf_op jit(solution)/shard_map/all_to_all | solution.py:20
  146.2 0.6 broadcast_in_dim.95
  146.8 3.2 %all-to-all-start.4 = ((f32[4,1,128]{2,1,0:T(1,128)}), f32[4,1,128]{2,1,0:T(1,128)S(1)}, u32[]{:S(2)}, u32[]{:S(2)}) async-start(f32[4,1,128]{2,1,0:T(1,128)} %broadcast_in_dim.95), calls=%async_computation.4 | async-start | bytes 4096 | tf_op jit(solution)/shard_map/all_to_all | solution.py:20
  150.0 9.9 %while.39 = (s32[]{:T(128)}, f32[128,512]{1,0:T(8,128)S(1)}, bf16[4096,512]{1,0:T(8,128)(2,1)}, bf16[256,512]{1,0:T(8,128)(2,1)S(1)}, f32[128]{0:T(128)S(1)}, /*...) while((s32[]{:T(128)}, f32[128,512]{1,0:T(8,128)S(1)}, ...), condition=%wide.region_13.14_spmd.clone, body=%wide.region_12.13_spmd.clone.sunk | while | flops 808105984 | bytes 9193157 | solution.py:113
  150.0 2.3 convolution_bitcast_fusion.7
  152.4 2.5 fusion.102
  155.0 2.3 convolution_bitcast_fusion.7
  157.3 2.5 fusion.102
  159.9 1.1 broadcast_in_dim.94
  161.0 4.7 %all-to-all-start.3 = ((f32[4,128,512]{2,1,0:T(8,128)}), f32[4,128,512]{2,1,0:T(8,128)S(1)}, u32[]{:S(2)}, u32[]{:S(2)}) async-start(f32[4,128,512]{2,1,0:T(8,128)} %broadcast_in_dim.94), calls=%async_computation.3 | async-start | bytes 2097152 | tf_op jit(solution)/shard_map/all_to_all | solution.py:20
  165.8 0.6 subtract_reduce_fusion
  166.4 15.3 %all-to-all-done.3 = f32[4,128,512]{2,1,0:T(8,128)S(1)} async-done(((f32[4,128,512]{2,1,0:T(8,128)}), f32[4,128,512]{2,1,0:T(8,128)S(1)}, u32[]{:S(2)}, u32[]{:S(2)}) %all-to-all-start.3) | async-done | bytes 1048608 | tf_op jit(solution)/shard_map/all_to_all | solution.py:20
  182.1 0.2 convolution_bitcast_fusion.3
  182.4 0.5 convolution_bitcast_fusion.2
  183.1 0.7 select_maximum_fusion
  183.8 0.9 reshape_reshape.10
  184.8 12.6 %all_to_all.61 = f32[2,64,1281]{2,1,0:T(8,128)S(1)} all-to-all(f32[2,64,1281]{2,1,0:T(8,128)S(1)} %copy.30), channel_id=1, replica_groups=mesh['wide_0'=4,'wide_1'=16,'wide_2'=2,'mp'=4] {'wide_2'}, dimensions={0} | all-to-all | bytes 1311744 | tf_op jit(solution)/shard_map/all_to_all | solution.py:68
  197.4 0.2 all_to_all.45
  197.7 34.7 %all_to_all.62 = f32[64,1,1281]{2,1,0:T(1,128)S(1)} all-to-all(f32[64,1,1281]{2,1,0:T(1,128)S(1)} %all_to_all.45), channel_id=1, replica_groups=mesh['wide_0'=4,'wide_1'=16,'wide_2'=2,'mp'=4] {'wide_0','wide_1'}, dimensions={0} | all-to-all | bytes 655872 | tf_op jit(solution)/shard_map/all_to_all | solution.py:76
  232.4 0.2 reduce_sum.193
  232.6 0.2 broadcast_in_dim.97
  232.8 29.9 %all_to_all.63 = f32[64,1,1281]{2,1,0:T(1,128)S(1)} all-to-all(f32[64,1,1281]{2,1,0:T(1,128)S(1)} %broadcast_in_dim.97), channel_id=1, replica_groups=mesh['wide_0'=4,'wide_1'=16,'wide_2'=2,'mp'=4] {'wide_0','wide_1'}, dimensions={0} | all-to-all | bytes 655872 | tf_op jit(solution)/shard_map/all_to_all | solution.py:20
  262.8 10.1 %all_to_all.64 = f32[2,64,1281]{2,1,0:T(8,128)S(1)} all-to-all(f32[2,64,1281]{2,1,0:T(8,128)S(1)} %broadcast_in_dim.99), channel_id=1, replica_groups=mesh['wide_0'=4,'wide_1'=16,'wide_2'=2,'mp'=4] {'wide_2'}, dimensions={0} | all-to-all | bytes 1311744 | tf_op jit(solution)/shard_map/all_to_all | solution.py:20
  272.8 0.6 copy.31
  273.4 0.6 reshape_reshape.11
  274.0 0.6 slice.57
  274.7 0.5 slice.68
  275.2 0.8 slice.69
  276.0 0.7 reshape.142
  (50 shorter events, 1.8 us)
Async XLA Ops:
  7.2 21.9 %copy-start = (bf16[128,768]{1,0:T(8,128)(2,1)S(1)}, bf16[128,768]{1,0:T(8,128)(2,1)}, u32[]{:S(2)}) copy-start(bf16[128,768]{1,0:T(8,128)(2,1)} %param.10) | copy-start | bytes 589828
  7.2 23.1 %copy-start.2 = (bf16[128,512]{1,0:T(8,128)(2,1)S(1)}, bf16[128,512]{1,0:T(8,128)(2,1)}, u32[]{:S(2)}) copy-start(bf16[128,512]{1,0:T(8,128)(2,1)} %param.14) | copy-start | bytes 393220
  7.2 102.4 %all-gather.5.cloned.1.call-start = ((), (), s32[]{:S(2)}) async-start(), calls=%async_computation.10 | async-start | bytes 4456448 | tf_op jit(solution)/shard_map/all_gather | solution.py:38
  30.3 4.9 %copy-start.1 = (bf16[128,512]{1,0:T(8,128)(2,1)S(1)}, bf16[128,512]{1,0:T(8,128)(2,1)}, u32[]{:S(2)}) copy-start(bf16[128,512]{1,0:T(8,128)(2,1)} %param.11) | copy-start | bytes 393220
  31.6 19.5 %all-to-all-start = ((f32[4,128,512]{2,1,0:T(8,128)}), f32[4,128,512]{2,1,0:T(8,128)S(1)}, u32[]{:S(2)}, u32[]{:S(2)}) async-start(f32[4,128,512]{2,1,0:T(8,128)} %broadcast_in_dim.90), calls=%async_computation | async-start | bytes 2097152 | tf_op jit(solution)/shard_map/all_to_all | solution.py:20
  109.6 4.8 %copy-start.3 = (s32[128]{0:T(128)S(1)}, s32[128]{0:T(128)}, u32[]{:S(2)}) copy-start(s32[128]{0:T(128)} %param.15) | copy-start | bytes 1540
  137.8 8.4 %all-to-all-start.5 = ((f32[4,1,128]{2,1,0:T(1,128)}), f32[4,1,128]{2,1,0:T(1,128)S(1)}, u32[]{:S(2)}, u32[]{:S(2)}) async-start(f32[4,1,128]{2,1,0:T(1,128)} %broadcast_in_dim.96), calls=%async_computation.5 | async-start | bytes 4096 | tf_op jit(solution)/shard_map/all_to_all | solution.py:20
  146.8 13.1 %all-to-all-start.4 = ((f32[4,1,128]{2,1,0:T(1,128)}), f32[4,1,128]{2,1,0:T(1,128)S(1)}, u32[]{:S(2)}, u32[]{:S(2)}) async-start(f32[4,1,128]{2,1,0:T(1,128)} %broadcast_in_dim.95), calls=%async_computation.4 | async-start | bytes 4096 | tf_op jit(solution)/shard_map/all_to_all | solution.py:20
  161.0 20.7 %all-to-all-start.3 = ((f32[4,128,512]{2,1,0:T(8,128)}), f32[4,128,512]{2,1,0:T(8,128)S(1)}, u32[]{:S(2)}, u32[]{:S(2)}) async-start(f32[4,128,512]{2,1,0:T(8,128)} %broadcast_in_dim.94), calls=%async_computation.3 | async-start | bytes 2097152 | tf_op jit(solution)/shard_map/all_to_all | solution.py:20
Sparse Core Ops, SparseCore 0:
  29.2 80.3 all-gather.4
where the time goes:
time: 286 us; the launch traced here: 285 us
  blocking collectives  124 us (43%)
  waiting for transfers between devices  94.2 us (33%)
  matrix products  16.5 us (6%)
  between operations  16.1 us (6%)
  starting transfers between devices  14.7 us (5%)
  local copies, waits for them, and re-layouts  13.7 us (5%)
  other arithmetic  5.68 us (2%)
    all_gather x1, waiting for transfers between devices, all_blocks(): parts = lax.all_gather(parts, axes[k])  58.2 us
    all_to_all x4, blocking collectives, from_everyone(): lax.all_to_all(jnp.broadcast_to(array[None], (devices, *array.shape)), ax...  56.9 us
    all_to_all x4, waiting for transfers between devices, from_everyone(): lax.all_to_all(jnp.broadcast_to(array[None], (devices, *array.shape)), ax...  36.1 us
    all_to_all x1, blocking collectives, summed_rows(): lax.all_to_all(nearer, far, split_axis=0, concat_axis=0, tiled=True)  34.7 us
    all_gather x2, blocking collectives, all_blocks(): parts = lax.all_gather(parts, axes[k])  19.9 us
    all_to_all x4, starting transfers between devices, from_everyone(): lax.all_to_all(jnp.broadcast_to(array[None], (devices, *array.shape)), ax...  14.7 us
    all_to_all x1, blocking collectives, summed_on_arrival(): lax.all_to_all(split_up(array, dim, devices), axis, 0, 0, tiled=True)  12.6 us
    dot_general x4, matrix products, inner_rows(): lax.dot_general(left, right, (((1,), (1,)), ((), ())), preferred_element_...  9.32 us
  transfers between devices with their start and end apart: 5, of which 4 were waited for; matrix products, arithmetic and copies ran while one was open for 5% of the time, Pallas kernels for 0%

commit v1 on v0

v1 whole, which is shorter than its diff:
```python
import jax
import jax.numpy as jnp
from jax import lax
from jax.experimental import pallas as pl
from jax.experimental.pallas import tpu as pltpu
from jax.sharding import Mesh
from jax.sharding import PartitionSpec as P

MESH = pl.DeviceIdType.MESH
WIDE = ("y", "z", "xl")
F32 = jnp.float32
BF16 = jnp.bfloat16

Y, Z, XL, MP = 4, 16, 2, 4
LINE = XL * MP
TEACHER_SCALE = 14.0
STUDENT_SCALE = 64.0
EPS = 1e-6
TILES = 10


def dot_nt(left, right, precision=None):
    return lax.dot_general(
        left, right, (((1,), (1,)), ((), ())), preferred_element_type=F32, precision=precision
    )


def normalize(values):
    return values / jnp.sqrt(jnp.sum(values * values, axis=1, keepdims=True) + EPS)


def rows(start, size):
    return pl.ds(pl.multiple_of(start, size), size)


def kernel(
    clip_h, ta_h, tt_h, w1_h, w2_h, pair_h,
    loss_o, gf_o, gs_o,
    clip_v, ta_v, tt_v, w1_v, w2_v, pair_v,
    A, B, C, stk, prow, pcol, rawp, rawr, st32, nm32, gprime, hid_v,
    ET, ES, acc, stat, statr, dp, dpb, rsr, drw,
    lossy, lossyr, lossz, losszr,
    gsb, gfb, p1s, p1f, own1, T, p2r, R, RR,
    sem_in, sA, rA, sB, rB, sB0, rB0, sC, rC,
    s_raw, r_raw, s_stud, r_stud, s_tp, r_tp, s_stat, r_stat, s_rs, r_rs, s_dr, r_dr,
    s_ly, r_ly, s_lz, r_lz, s_p1, r_p1, s_p2, r_p2, s_p3, r_p3, s_p4, r_p4,
):
    y, z = lax.axis_index("y"), lax.axis_index("z")
    xl, mp = lax.axis_index("xl"), lax.axis_index("mp")
    q = xl * MP + mp
    j = y * XL + xl
    total = 128 * Y * Z * XL

    def rem(v, n):
        return lax.rem(v + 4 * n, n)

    def y_peer(e):
        return (rem(y + e, Y), z, xl, mp)

    def z_peer(e):
        return (y, rem(z + e, Z), xl, mp)

    def line_peer(e):
        other = rem(q + e, LINE)
        return (y, z, other // MP, rem(other, MP))

    def mp_peer(e):
        return (y, z, xl, rem(mp + e, MP))

    def group_peer(e):
        other = rem(j + e, Y * XL)
        return (other // XL, z, rem(other, XL), mp)

    def remote(src, dst, send, recv, to):
        return pltpu.make_async_remote_copy(
            src_ref=src, dst_ref=dst, send_sem=send, recv_sem=recv, device_id=to,
            device_id_type=MESH,
        )

    me = (y, z, xl, mp)
    sends = []

    def push(*args):
        copy = remote(*args)
        copy.start()
        sends.append(copy)

    def arrived(dst, recv):
        remote(dst, dst, recv, recv, me).wait_recv()

    ins = [
        pltpu.make_async_copy(h, v, sem_in.at[i])
        for i, (h, v) in enumerate(
            [(tt_h, tt_v), (clip_h, clip_v), (w1_h, w1_v), (w2_h, w2_v), (ta_h, ta_v), (pair_h, pair_v)]
        )
    ]
    for c in ins:
        c.start()
    barrier = pltpu.get_barrier_semaphore()
    partners = [line_peer(e) for e in range(1, LINE)]
    partners += [y_peer(e) for e in range(1, Y)] + [z_peer(1), z_peer(-1)]
    for p in partners:
        pl.semaphore_signal(barrier, inc=1, device_id=p, device_id_type=MESH)
    ins[0].wait()
    A[0, 0] = normalize(tt_v[...].astype(F32)).astype(BF16)
    pl.semaphore_wait(barrier, len(partners))

    for e in (1, 3, 2):
        push(A.at[0, 0, pl.ds(0, 16)], B.at[0, 0, 3 - e], sB0.at[3 - e], rB0.at[3 - e], y_peer(e))
    push(A.at[0, 0], A.at[1, 0], sA.at[1, 0], rA.at[1, 0], z_peer(1))
    push(A.at[0, 0], A.at[1, 1], sA.at[1, 1], rA.at[1, 1], z_peer(-1))
    for e in (1, 3, 2):
        push(A.at[0, 0, pl.ds(16, 16)], C.at[0, 3 - e, 0], sC.at[0, 3 - e], rC.at[0, 3 - e], y_peer(e))

    for c in ins[1:4]:
        c.wait()
    pre = jnp.dot(clip_v[...], w1_v[...], preferred_element_type=F32)
    cdf = 0.5 * (1.0 + lax.erf(pre * 0.7071067811865476))
    hid = (pre * cdf).astype(BF16)
    hid_v[...] = hid
    rawp[...] = jnp.dot(hid, w2_v[...], preferred_element_type=F32)
    for e in (2, 1, 3):
        other = rem(mp + e, MP)
        push(rawp.at[rows(other * 32, 32)], rawr.at[e - 1], s_raw.at[e - 1], r_raw.at[e - 1], mp_peer(e))
    for e in range(1, Y):
        arrived(B.at[0, 0, 3 - e], rB0.at[3 - e])
    push(B.at[0, 0], B.at[1, 0], sB.at[1, 0], rB.at[1, 0], z_peer(1))
    push(B.at[0, 0], B.at[1, 1], sB.at[1, 1], rB.at[1, 1], z_peer(-1))
    ins[4].wait()
    ins[5].wait()
    mine = rows(xl * 128, 128)
    stk[mine] = normalize(ta_v[...].astype(F32)).astype(BF16)
    prow[xl] = jnp.broadcast_to(pair_v[...], (8, 128))
    other_x = (y, z, 1 - xl, mp)
    push(stk.at[mine], stk.at[mine], s_tp.at[0], r_tp.at[0], other_x)
    push(prow.at[xl], prow.at[xl], s_tp.at[1], r_tp.at[1], other_x)
    gprime[...] = cdf + pre * (0.3989422804014327 * jnp.exp(-0.5 * pre * pre))

    def comm(k):
        for d, way in ((0, 1), (1, -1)):
            arrived(A.at[k, d], rA.at[k, d])
            if k < 7:
                push(A.at[k, d], A.at[k + 1, d], sA.at[k + 1, d], rA.at[k + 1, d], z_peer(way))
            elif d == 0:
                push(A.at[k, d], A.at[0, 1], sA.at[0, 1], rA.at[0, 1], z_peer(way))
        for e in (1, 3, 2):
            push(
                A.at[k, :, pl.ds(16, 16)], C.at[k, 3 - e], sC.at[k, 3 - e], rC.at[k, 3 - e],
                y_peer(e),
            )
        for d, way in ((0, 1), (1, -1)):
            arrived(B.at[k, d], rB.at[k, d])
            if k < 7:
                push(B.at[k, d], B.at[k + 1, d], sB.at[k + 1, d], rB.at[k + 1, d], z_peer(way))
            elif d == 1:
                push(B.at[k, d], B.at[0, 1], sB.at[0, 1], rB.at[0, 1], z_peer(way))

    def far():
        arrived(A.at[0, 1], rA.at[0, 1])
        for e in (1, 3, 2):
            push(
                A.at[0, 1, pl.ds(16, 16)], C.at[0, 3 - e, 1], sC.at[8, 3 - e], rC.at[8, 3 - e],
                y_peer(e),
            )
        arrived(B.at[0, 1], rB.at[0, 1])

    col = lax.broadcasted_iota(jnp.int32, (8, 256), 1)
    in_a, in_b = col < 64, col < 160
    b_way = (col >= 112).astype(jnp.int32)
    b_at = col - 64 - 48 * b_way
    b_off = 1 + (b_at >= 16).astype(jnp.int32) + (b_at >= 32).astype(jnp.int32)
    c_at = col - 160
    c_off = 1 + (c_at >= 32).astype(jnp.int32) + (c_at >= 64).astype(jnp.int32)
    way = jnp.where(in_a, (col >= 32).astype(jnp.int32), jnp.where(in_b, b_way, (c_at & 16) // 16))
    y_off = jnp.where(in_a, 0, jnp.where(in_b, b_off, c_off))
    line = jnp.where(in_a, col & 31, jnp.where(in_b, b_at & 15, 16 + (c_at & 15)))
    y_at = (y + y_off) & (Y - 1)
    id_base = ((y_at * Z) * XL + xl) * 128 + mp * 32 + line

    def hits(k):
        z_left = rem(z - k, Z)
        z_right = jnp.where(k == 0, rem(z + 8, Z), rem(z + k, Z))
        ids = id_base + jnp.where(way == 1, z_right, z_left) * (XL * 128)
        ids = ids[0:1].astype(F32)
        return [pcol[...] == ids[:, h * 128 : (h + 1) * 128] for h in (0, 1)]

    def captions(k):
        return jnp.concatenate(
            [A[k].reshape(64, 512), B[k].reshape(96, 512), C[k].reshape(96, 512)], axis=0
        )

    def chunk(k):
        scores = dot_nt(stk[...], captions(k))
        tlog = TEACHER_SCALE * scores[:256]
        slog = STUDENT_SCALE * scores[256:]
        texp, sexp = jnp.exp(tlog), jnp.exp(slog)
        ET[k] = texp
        ES[k] = sexp
        lean = texp * (tlog - slog)
        hit = hits(k)
        pair = [jnp.where(hit[h], slog[:, h * 128 : (h + 1) * 128], 0.0) for h in (0, 1)]
        acc[0] += texp[:, :128] + texp[:, 128:]
        acc[1] += sexp[:, :128] + sexp[:, 128:]
        acc[2] += lean[:, :128] + lean[:, 128:]
        acc[3] += pair[0] + pair[1]

    def c_arrived(k):
        for d in range(3):
            arrived(C.at[k, d], rC.at[k, d])

    acc[...] = jnp.zeros_like(acc)
    comm(1)
    for e in range(1, MP):
        arrived(rawr.at[e - 1], r_raw.at[e - 1])
    raw = rawp[rows(mp * 32, 32)] + rawr[0] + rawr[1] + rawr[2]
    norm = jnp.sqrt(jnp.sum(raw * raw, axis=1, keepdims=True) + EPS)
    student = raw / norm
    st32[...] = student
    nm32[...] = jnp.broadcast_to(norm, (32, 128))
    own = rows(256 + q * 32, 32)
    stk[own] = student.astype(BF16)
    for e in range(1, LINE):
        push(stk.at[own], stk.at[own], s_stud.at[e - 1], r_stud.at[e - 1], line_peer(e))
    comm(2)
    theirs = rows((1 - xl) * 128, 128)
    arrived(stk.at[theirs], r_tp.at[0])
    arrived(prow.at[1 - xl], r_tp.at[1])
    for i in range(XL):
        one = jnp.broadcast_to(prow[i][0:1].astype(F32), (128, 128))
        pcol[pl.ds(i * 128, 128)] = one.T
    comm(3)
    for e in range(1, LINE):
        arrived(stk.at[rows(256 + rem(q - e, LINE) * 32, 32)], r_stud.at[e - 1])
    for k in range(4, 8):
        comm(k)
        c_arrived(k - 3)
        chunk(k - 3)
    far()
    for k in range(5, 8):
        c_arrived(k)
        chunk(k)
    for d in range(3):
        arrived(C.at[0, d, 0], rC.at[0, d])
        arrived(C.at[0, d, 1], rC.at[8, d])
    chunk(0)

    pick = (
        lax.broadcasted_iota(jnp.int32, (8, 512), 0)
        == lax.broadcasted_iota(jnp.int32, (8, 512), 1) // 128
    ).astype(F32)
    stat[...] = dot_nt(
        pick, jnp.concatenate([acc[i] for i in range(4)], axis=1), lax.Precision.HIGHEST
    )
    for e in range(1, LINE):
        push(stat, statr.at[e - 1], s_stat.at[e - 1], r_stat.at[e - 1], line_peer(e))
    for e in range(1, LINE):
        arrived(statr.at[e - 1], r_stat.at[e - 1])
    sums = stat[...]
    for e in range(1, LINE):
        sums = sums + statr[e - 1]
    zt, zs, lean, pair = (sums[i : i + 1] for i in range(4))
    part = jnp.sum(lean / zt - jnp.log(zt) + 2.0 * jnp.log(zs) - pair, axis=1, keepdims=True)
    lossy[...] = jnp.broadcast_to(part, (8, 128))
    for e in range(1, Y):
        push(lossy, lossyr.at[e - 1], s_ly.at[e - 1], r_ly.at[e - 1], y_peer(e))
    c_t = jnp.broadcast_to(1.0 / zt, (128, 256)).T
    c_s = jnp.broadcast_to(2.0 / zs, (128, 256)).T

    for k in range(8):
        hit = hits(k)
        coef = jnp.concatenate(
            [
                (
                    ES[k, :, h * 128 : (h + 1) * 128] * c_s
                    - ET[k, :, h * 128 : (h + 1) * 128] * c_t
                    - hit[h].astype(F32)
                ).astype(BF16)
                for h in (0, 1)
            ],
            axis=1,
        )
        more = jnp.dot(coef, captions(k), preferred_element_type=F32)
        if k == 0:
            dp[...] = more
        else:
            dp[...] += more
    dpb[...] = dp[...].astype(BF16)
    for e in (3, 5, 4, 1, 7, 2, 6):
        other = rem(q + e, LINE)
        push(dpb.at[rows(other * 32, 32)], rsr.at[e - 1], s_rs.at[e - 1], r_rs.at[e - 1], line_peer(e))
    for e in range(1, Y):
        arrived(lossyr.at[e - 1], r_ly.at[e - 1])
    lossz[...] = lossy[...] + lossyr[0] + lossyr[1] + lossyr[2]
    for e in range(1, Z):
        push(lossz, losszr.at[e - 1], s_lz.at[e - 1], r_lz.at[e - 1], z_peer(e))
    dstud = dp[rows(q * 32, 32)]
    for e in range(1, LINE):
        arrived(rsr.at[e - 1], r_rs.at[e - 1])
        dstud = dstud + rsr[e - 1].astype(F32)
    dstud = dstud * (STUDENT_SCALE / total)
    student = st32[...]
    inner = jnp.sum(student * dstud, axis=1, keepdims=True)
    own = rows(mp * 32, 32)
    drw[own] = ((dstud - student * inner) / nm32[:, 0:1]).astype(BF16)
    for e in (2, 1, 3):
        push(drw.at[own], drw.at[own], s_dr.at[e - 1], r_dr.at[e - 1], mp_peer(e))
    for e in range(1, MP):
        arrived(drw.at[rows(rem(mp - e, MP) * 32, 32)], r_dr.at[e - 1])

    draw = drw[...]
    gs = lax.dot_general(
        hid_v[...], draw, (((0,), (0,)), ((), ())), preferred_element_type=F32
    )
    gsb[...] = gs.astype(BF16)
    group = Y * XL
    for e in range(1, group):
        other = rem(j + e, group)
        push(gsb.at[rows(other * 16, 16)], p1s.at[e - 1], s_p1.at[0, e - 1], r_p1.at[0, e - 1], group_peer(e))
    gs_o[...] = gs
    dpre = (dot_nt(draw, w2_v[...]) * gprime[...]).astype(BF16)
    gf = lax.dot_general(
        clip_v[...], dpre, (((0,), (0,)), ((), ())), preferred_element_type=F32
    )
    gfb[...] = gf.astype(BF16)
    for e in range(1, group):
        other = rem(j + e, group)
        push(gfb.at[rows(other * 96, 96)], p1f.at[e - 1], s_p1.at[1, e - 1], r_p1.at[1, e - 1], group_peer(e))
    gf_o[...] = gf
    one_s = gs_o[rows(j * 16, 16)]
    one_f = gf_o[rows(j * 96, 96)]
    for e in range(1, group):
        arrived(p1s.at[e - 1], r_p1.at[0, e - 1])
        one_s = one_s + p1s[e - 1].astype(F32)
    for e in range(1, group):
        arrived(p1f.at[e - 1], r_p1.at[1, e - 1])
        one_f = one_f + p1f[e - 1].astype(F32)
    own1[pl.ds(0, 96)] = one_f
    for i in range(4):
        own1[pl.ds(96 + 16 * i, 16)] = one_s[:, i * 128 : (i + 1) * 128]
    T[...] = own1[...].astype(BF16)
    for t in range(TILES):

        @pl.when(z != t)
        def _():
            slot = rem(z - t, Z) - 1
            remote(
                T.at[pl.ds(16 * t, 16)], p2r.at[slot], s_p2.at[t], r_p2.at[slot], (y, t, xl, mp)
            ).start()

    loss_sum = lossz[...]
    for e in range(1, Z):
        arrived(losszr.at[e - 1], r_lz.at[e - 1])
        loss_sum = loss_sum + losszr[e - 1]
    loss_o[0, 0] = jnp.sum(loss_sum[0:1, 0:1]) / total

    @pl.when(z < TILES)
    def _():
        tile = rows(z * 16, 16)
        out = own1[tile]
        for e in range(1, Z):
            arrived(p2r.at[e - 1], r_p2.at[e - 1])
            out = out + p2r[e - 1].astype(F32)
        R[tile] = out.astype(BF16)
        for e in range(1, Z):
            remote(R.at[tile], R.at[tile], s_p3.at[e - 1], r_p3.at[z], z_peer(e)).start()

    for t in range(TILES):

        @pl.when(z != t)
        def _():
            arrived(R.at[pl.ds(16 * t, 16)], r_p3.at[t])

    for e in range(1, group):
        push(R, RR.at[e - 1], s_p4.at[e - 1], r_p4.at[e - 1], group_peer(e))

    def write(owner, ref):
        gf_o[rows(owner * 96, 96)] = ref[pl.ds(0, 96)].astype(F32)
        for i in range(4):
            gs_o[rows(owner * 16, 16), i * 128 : (i + 1) * 128] = ref[
                pl.ds(96 + 16 * i, 16)
            ].astype(F32)

    write(j, R)
    for e in range(1, group):
        arrived(RR.at[e - 1], r_p4.at[e - 1])
        write(rem(j - e, group), RR.at[e - 1])

    for copy in sends:
        copy.wait_send()
    for t in range(TILES):

        @pl.when(z != t)
        def _():
            remote(T.at[pl.ds(16 * t, 16)], T.at[pl.ds(16 * t, 16)], s_p2.at[t], s_p2.at[t], me).wait_send()

    @pl.when(z < TILES)
    def _():
        tile = rows(z * 16, 16)
        for e in range(1, Z):
            remote(R.at[tile], R.at[tile], s_p3.at[e - 1], s_p3.at[e - 1], me).wait_send()


def body(clip_feats, teacher_audio, teacher_text, w_first, w_second, pairing):
    vm = pltpu.VMEM
    dma = pltpu.SemaphoreType.DMA
    hbm = pl.BlockSpec(memory_space=pl.ANY)
    scratch = [
        vm((128, 768), BF16), vm((128, 512), BF16), vm((32, 512), BF16),
        vm((768, 128), BF16), vm((128, 512), BF16), vm((1, 128), jnp.int32),
        vm((8, 2, 32, 512), BF16), vm((8, 2, 3, 16, 512), BF16), vm((8, 3, 2, 16, 512), BF16),
        vm((512, 512), BF16), vm((2, 8, 128), jnp.int32), vm((256, 128), F32),
        vm((128, 512), F32), vm((3, 32, 512), F32), vm((32, 512), F32), vm((32, 128), F32),
        vm((128, 128), F32), vm((128, 128), BF16),
        vm((8, 256, 256), F32), vm((8, 256, 256), F32), vm((4, 256, 128), F32),
        vm((8, 256), F32), vm((7, 8, 256), F32),
        vm((256, 512), F32), vm((256, 512), BF16), vm((7, 32, 512), BF16), vm((128, 512), BF16),
        vm((8, 128), F32), vm((3, 8, 128), F32), vm((8, 128), F32), vm((15, 8, 128), F32),
        vm((128, 512), BF16), vm((768, 128), BF16), vm((7, 16, 512), BF16), vm((7, 96, 128), BF16),
        vm((160, 128), F32), vm((160, 128), BF16), vm((15, 16, 128), BF16),
        vm((160, 128), BF16), vm((7, 160, 128), BF16),
        dma((6,)), dma((8, 2)), dma((8, 2)), dma((8, 2)), dma((8, 2)), dma((3,)), dma((3,)),
        dma((9, 3)), dma((9, 3)),
        dma((3,)), dma((3,)), dma((7,)), dma((7,)), dma((2,)), dma((2,)), dma((7,)), dma((7,)),
        dma((7,)), dma((7,)), dma((3,)), dma((3,)),
        dma((3,)), dma((3,)), dma((15,)), dma((15,)), dma((2, 7)), dma((2, 7)),
        dma((TILES,)), dma((15,)), dma((15,)), dma((TILES,)), dma((7,)), dma((7,)),
    ]
    loss, grad_first, grad_second = pl.pallas_call(
        kernel,
        out_shape=(
            jax.ShapeDtypeStruct((1, 1), F32),
            jax.ShapeDtypeStruct((768, 128), F32),
            jax.ShapeDtypeStruct((128, 512), F32),
        ),
        in_specs=[hbm] * 6,
        out_specs=(
            pl.BlockSpec(memory_space=pltpu.SMEM),
            pl.BlockSpec(memory_space=pltpu.VMEM),
            pl.BlockSpec(memory_space=pltpu.VMEM),
        ),
        scratch_shapes=scratch,
        compiler_params=pltpu.CompilerParams(
            collective_id=0, has_side_effects=True, vmem_limit_bytes=48 * 1024 * 1024
        ),
    )(clip_feats, teacher_audio, teacher_text, w_first, w_second, pairing.reshape(1, 128))
    return loss.reshape(()), grad_first, grad_second


def solution(mesh):
    finer = Mesh(mesh.devices.reshape(Y, Z, XL, MP), ("y", "z", "xl", "mp"))
    return jax.shard_map(
        body,
        mesh=finer,
        in_specs=(
            P(WIDE, None),
            P(WIDE, None),
            P(WIDE + ("mp",), None),
            P(None, "mp"),
            P("mp", None),
            P(WIDE),
        ),
        out_specs=(P(), P(None, "mp"), P("mp", None)),
        check_vma=False,
    )
```

time: 286 us -> 103 us (0.36)
  blocking collectives: 124 us -> 0 us
  waiting for transfers between devices: 94.2 us -> 0 us
  Pallas kernels: 0 us -> 92.2 us
  matrix products: 16.5 us -> 0 us
  starting transfers between devices: 14.7 us -> 0 us
  between operations: 16.1 us -> 2.47 us
  local copies, waits for them, and re-layouts: 13.7 us -> 6.52 us
  other arithmetic: 5.68 us -> 0 us
    all_to_all x6 -> x0, blocking collectives: 104 us -> none  [the longest x4 56.9 us: from_everyone(): lax.all_to_all(jnp.broadcast_to(array[None], (devices, *array.shape)), ax...]
    pallas_call x0 -> x1, Pallas kernels: none -> 92.2 us  [body(): pl.pallas_call(kernel, out_shape=(jax.ShapeDtypeStruct((1, 1), F32), jax....]
    all_gather x1 -> x0, waiting for transfers between devices: 58.2 us -> none  [all_blocks(): parts = lax.all_gather(parts, axes[k])]
    all_to_all x4 -> x0, waiting for transfers between devices: 36.1 us -> none  [from_everyone(): lax.all_to_all(jnp.broadcast_to(array[None], (devices, *array.shape)), ax...]
    all_gather x2 -> x0, blocking collectives: 19.9 us -> none  [all_blocks(): parts = lax.all_gather(parts, axes[k])]
    dot_general x10 -> x0, matrix products: 16.5 us -> none  [the longest x4 9.32 us: inner_rows(): lax.dot_general(left, right, (((1,), (1,)), ((), ())), preferred_element_...]
    all_to_all x4 -> x0, starting transfers between devices: 14.7 us -> none  [from_everyone(): lax.all_to_all(jnp.broadcast_to(array[None], (devices, *array.shape)), ax...]
    unnamed x10 -> x14, local copies, waits for them, and re-layouts: 0.12 us -> 6.52 us
  transfers between devices with their start and end apart: 5 -> 0, of which waited for: 4 -> 0; matrix products, arithmetic and copies ran while one was open for 5% -> 0% of each run, Pallas kernels for 0% -> 0%
where the time goes in v1:
time: 103 us; the launch traced here: 101 us
  Pallas kernels  92.2 us (90%)
  local copies, waits for them, and re-layouts  6.52 us (6%)
  between operations  2.47 us (2%)
    pallas_call x1, Pallas kernels, body(): pl.pallas_call(kernel, out_shape=(jax.ShapeDtypeStruct((1, 1), F32), jax....  92.2 us
    unnamed x14, local copies, waits for them, and re-layouts  6.52 us

profile of v1, /device:TPU:24, one launch (start us, length us, event | category | flops | bytes accessed | tf_op | source)
XLA Modules:
  0.0 101.2 jit_solution(16137127958155699049)
XLA Ops:
  0.6 0.0 copy-start.5
  0.6 0.6 copy-done.5
  1.3 0.0 copy-start
  1.3 0.9 copy-done
  2.2 0.0 copy-start.1
  2.2 0.9 copy-done.1
  3.1 0.0 copy-start.2
  3.1 0.9 copy-done.2
  4.0 0.0 copy-start.3
  4.0 0.9 copy-done.3
  5.0 0.0 copy-start.4
  5.0 0.8 copy-done.4
  5.7 92.2 %shard_map.85 = (f32[1,1]{1,0:T(1,128)}, f32[768,128]{1,0:T(8,128)S(1)}, f32[128,512]{1,0:T(8,128)S(1)}) custom-call(bf16[128,768]{1,0:T(8,128)(2,1)S(1)} %copy-done, bf16[128,512]{1,0:T(8,128)(2,1)S(1)} %copy-done.2, bf16[32,512]{1,0:T(8,128)(2,1)S(1)} %copy-done.4, bf16[768,128]{1,0:T(8,128)(2,1)S(1)} %copy-done.1, bf16[128,512]{1,0:T(8,128)(2,1)S(1)} %copy-done.3, ...), custom_call_target="tpu_custom_call" | custom-call | tf_op jit(solution)/shard_map/pallas_call | solution.py:428
  98.6 0.7 copy.13
  99.3 0.7 copy.14
Async XLA Ops:
  0.6 0.7 copy-start.5
  1.3 0.9 copy-start
  2.2 0.9 copy-start.1
  3.1 0.9 copy-start.2
  4.0 0.9 copy-start.3
  5.0 0.8 copy-start.4

commit v2 on v1

--- a/solution.py
+++ b/solution.py
@@ -19,9 +19,9 @@
 TILES = 10
 
 
-def dot_nt(left, right, precision=None):
+def dot_nt(left, right):
     return lax.dot_general(
-        left, right, (((1,), (1,)), ((), ())), preferred_element_type=F32, precision=precision
+        left, right, (((1,), (1,)), ((), ())), preferred_element_type=F32
     )
 
 
@@ -37,11 +37,11 @@
     clip_h, ta_h, tt_h, w1_h, w2_h, pair_h,
     loss_o, gf_o, gs_o,
     clip_v, ta_v, tt_v, w1_v, w2_v, pair_v,
-    A, B, C, stk, prow, pcol, rawp, rawr, st32, nm32, gprime, hid_v,
+    G, stk, prow, pcol, rawp, rawr, st32, nm32, gprime, hid_v,
     ET, ES, acc, stat, statr, dp, dpb, rsr, drw,
     lossy, lossyr, lossz, losszr,
     gsb, gfb, p1s, p1f, own1, T, p2r, R, RR,
-    sem_in, sA, rA, sB, rB, sB0, rB0, sC, rC,
+    sem_in, sA, rA, sB, rB, sC, rC,
     s_raw, r_raw, s_stud, r_stud, s_tp, r_tp, s_stat, r_stat, s_rs, r_rs, s_dr, r_dr,
     s_ly, r_ly, s_lz, r_lz, s_p1, r_p1, s_p2, r_p2, s_p3, r_p3, s_p4, r_p4,
 ):
@@ -98,19 +98,32 @@
         c.start()
     barrier = pltpu.get_barrier_semaphore()
     partners = [line_peer(e) for e in range(1, LINE)]
-    partners += [y_peer(e) for e in range(1, Y)] + [z_peer(1), z_peer(-1)]
+    partners += [y_peer(e) for e in range(1, Y)] + [z_peer(e) for e in (1, -1, 2, -2)]
     for p in partners:
         pl.semaphore_signal(barrier, inc=1, device_id=p, device_id_type=MESH)
     ins[0].wait()
-    A[0, 0] = normalize(tt_v[...].astype(F32)).astype(BF16)
+    G[0, 0, 0] = normalize(tt_v[...].astype(F32)).astype(BF16)
     pl.semaphore_wait(barrier, len(partners))
 
-    for e in (1, 3, 2):
-        push(A.at[0, 0, pl.ds(0, 16)], B.at[0, 0, 3 - e], sB0.at[3 - e], rB0.at[3 - e], y_peer(e))
-    push(A.at[0, 0], A.at[1, 0], sA.at[1, 0], rA.at[1, 0], z_peer(1))
-    push(A.at[0, 0], A.at[1, 1], sA.at[1, 1], rA.at[1, 1], z_peer(-1))
-    for e in (1, 3, 2):
-        push(A.at[0, 0, pl.ds(16, 16)], C.at[0, 3 - e, 0], sC.at[0, 3 - e], rC.at[0, 3 - e], y_peer(e))
+    def along_z(o, k, d, send, recv):
+        way = 1 - 2 * d
+        for step in (2, 1):
+            slot, side = k + step, d
+            if slot == 8:
+                if d != o // 2:
+                    continue
+                slot, side = 0, 1
+            src = G.at[k, o, 0 if k == 0 else d]
+            push(src, G.at[slot, o, side], send.at[slot, side], recv.at[slot, side], z_peer(way * step))
+
+    def along_y(k, d):
+        for e in (1, 3):
+            push(G.at[k, 0, d], G.at[k, Y - e, d], sC.at[k, d, e // 2], rC.at[k, d, e // 2], y_peer(e))
+
+    push(G.at[0, 0, 0], G.at[0, 2, 0], sB.at[0, 0], rB.at[0, 0], y_peer(2))
+    for d in (0, 1):
+        along_z(0, 0, d, sA, rA)
+    along_y(0, 0)
 
     for c in ins[1:4]:
         c.wait()
@@ -122,10 +135,9 @@
     for e in (2, 1, 3):
         other = rem(mp + e, MP)
         push(rawp.at[rows(other * 32, 32)], rawr.at[e - 1], s_raw.at[e - 1], r_raw.at[e - 1], mp_peer(e))
-    for e in range(1, Y):
-        arrived(B.at[0, 0, 3 - e], rB0.at[3 - e])
-    push(B.at[0, 0], B.at[1, 0], sB.at[1, 0], rB.at[1, 0], z_peer(1))
-    push(B.at[0, 0], B.at[1, 1], sB.at[1, 1], rB.at[1, 1], z_peer(-1))
+    arrived(G.at[0, 2, 0], rB.at[0, 0])
+    for d in (0, 1):
+        along_z(2, 0, d, sB, rB)
     ins[4].wait()
     ins[5].wait()
     mine = rows(xl * 128, 128)
@@ -137,45 +149,26 @@
     gprime[...] = cdf + pre * (0.3989422804014327 * jnp.exp(-0.5 * pre * pre))
 
     def comm(k):
-        for d, way in ((0, 1), (1, -1)):
-            arrived(A.at[k, d], rA.at[k, d])
-            if k < 7:
-                push(A.at[k, d], A.at[k + 1, d], sA.at[k + 1, d], rA.at[k + 1, d], z_peer(way))
-            elif d == 0:
-                push(A.at[k, d], A.at[0, 1], sA.at[0, 1], rA.at[0, 1], z_peer(way))
-        for e in (1, 3, 2):
-            push(
-                A.at[k, :, pl.ds(16, 16)], C.at[k, 3 - e], sC.at[k, 3 - e], rC.at[k, 3 - e],
-                y_peer(e),
-            )
-        for d, way in ((0, 1), (1, -1)):
-            arrived(B.at[k, d], rB.at[k, d])
-            if k < 7:
-                push(B.at[k, d], B.at[k + 1, d], sB.at[k + 1, d], rB.at[k + 1, d], z_peer(way))
-            elif d == 1:
-                push(B.at[k, d], B.at[0, 1], sB.at[0, 1], rB.at[0, 1], z_peer(way))
+        for d in (0, 1):
+            arrived(G.at[k, 0, d], rA.at[k, d])
+            along_z(0, k, d, sA, rA)
+        for d in (0, 1):
+            arrived(G.at[k, 2, d], rB.at[k, d])
+            along_z(2, k, d, sB, rB)
+        for d in (0, 1):
+            arrived(G.at[k - 1, 0, d], rA.at[k - 1, d])
+            along_y(k - 1, d)
+            along_y(k, d)
 
     def far():
-        arrived(A.at[0, 1], rA.at[0, 1])
-        for e in (1, 3, 2):
-            push(
-                A.at[0, 1, pl.ds(16, 16)], C.at[0, 3 - e, 1], sC.at[8, 3 - e], rC.at[8, 3 - e],
-                y_peer(e),
-            )
-        arrived(B.at[0, 1], rB.at[0, 1])
+        for k, d in ((7, 0), (7, 1), (0, 1)):
+            arrived(G.at[k, 0, d], rA.at[k, d])
+            along_y(k, d)
 
     col = lax.broadcasted_iota(jnp.int32, (8, 256), 1)
-    in_a, in_b = col < 64, col < 160
-    b_way = (col >= 112).astype(jnp.int32)
-    b_at = col - 64 - 48 * b_way
-    b_off = 1 + (b_at >= 16).astype(jnp.int32) + (b_at >= 32).astype(jnp.int32)
-    c_at = col - 160
-    c_off = 1 + (c_at >= 32).astype(jnp.int32) + (c_at >= 64).astype(jnp.int32)
-    way = jnp.where(in_a, (col >= 32).astype(jnp.int32), jnp.where(in_b, b_way, (c_at & 16) // 16))
-    y_off = jnp.where(in_a, 0, jnp.where(in_b, b_off, c_off))
-    line = jnp.where(in_a, col & 31, jnp.where(in_b, b_at & 15, 16 + (c_at & 15)))
-    y_at = (y + y_off) & (Y - 1)
-    id_base = ((y_at * Z) * XL + xl) * 128 + mp * 32 + line
+    way = (col // 32) & 1
+    y_at = (y + col // 64) & (Y - 1)
+    id_base = ((y_at * Z) * XL + xl) * 128 + mp * 32 + (col & 31)
 
     def hits(k):
         z_left = rem(z - k, Z)
@@ -185,9 +178,7 @@
         return [pcol[...] == ids[:, h * 128 : (h + 1) * 128] for h in (0, 1)]
 
     def captions(k):
-        return jnp.concatenate(
-            [A[k].reshape(64, 512), B[k].reshape(96, 512), C[k].reshape(96, 512)], axis=0
-        )
+        return G[k].reshape(256, 512)
 
     def chunk(k):
         scores = dot_nt(stk[...], captions(k))
@@ -204,12 +195,15 @@
         acc[2] += lean[:, :128] + lean[:, 128:]
         acc[3] += pair[0] + pair[1]
 
-    def c_arrived(k):
-        for d in range(3):
-            arrived(C.at[k, d], rC.at[k, d])
+    def complete(k):
+        for d in (0, 1):
+            if k == 7 or (k in (1, 3, 5)) or (k == 0 and d == 1):
+                arrived(G.at[k, 2, d], rB.at[k, d])
+            for e in (1, 3):
+                arrived(G.at[k, Y - e, d], rC.at[k, d, e // 2])
 
     acc[...] = jnp.zeros_like(acc)
-    comm(1)
+    comm(2)
     for e in range(1, MP):
         arrived(rawr.at[e - 1], r_raw.at[e - 1])
     raw = rawp[rows(mp * 32, 32)] + rawr[0] + rawr[1] + rawr[2]
@@ -221,36 +215,29 @@
     stk[own] = student.astype(BF16)
     for e in range(1, LINE):
         push(stk.at[own], stk.at[own], s_stud.at[e - 1], r_stud.at[e - 1], line_peer(e))
-    comm(2)
+    comm(4)
     theirs = rows((1 - xl) * 128, 128)
     arrived(stk.at[theirs], r_tp.at[0])
     arrived(prow.at[1 - xl], r_tp.at[1])
     for i in range(XL):
         one = jnp.broadcast_to(prow[i][0:1].astype(F32), (128, 128))
         pcol[pl.ds(i * 128, 128)] = one.T
-    comm(3)
+    comm(6)
     for e in range(1, LINE):
         arrived(stk.at[rows(256 + rem(q - e, LINE) * 32, 32)], r_stud.at[e - 1])
-    for k in range(4, 8):
-        comm(k)
-        c_arrived(k - 3)
-        chunk(k - 3)
+    for k in (1, 2):
+        complete(k)
+        chunk(k)
     far()
-    for k in range(5, 8):
-        c_arrived(k)
+    for k in (3, 4, 5, 6, 7, 0):
+        complete(k)
         chunk(k)
-    for d in range(3):
-        arrived(C.at[0, d, 0], rC.at[0, d])
-        arrived(C.at[0, d, 1], rC.at[8, d])
-    chunk(0)
-
-    pick = (
-        lax.broadcasted_iota(jnp.int32, (8, 512), 0)
-        == lax.broadcasted_iota(jnp.int32, (8, 512), 1) // 128
-    ).astype(F32)
-    stat[...] = dot_nt(
-        pick, jnp.concatenate([acc[i] for i in range(4)], axis=1), lax.Precision.HIGHEST
-    )
+
+    lane = lax.broadcasted_iota(jnp.int32, (256, 128), 1)
+    cols = jnp.zeros((256, 128), F32)
+    for i in range(4):
+        cols = jnp.where(lane == i, jnp.sum(acc[i], axis=1, keepdims=True), cols)
+    stat[...] = cols.T[0:8]
     for e in range(1, LINE):
         push(stat, statr.at[e - 1], s_stat.at[e - 1], r_stat.at[e - 1], line_peer(e))
     for e in range(1, LINE):
@@ -259,10 +246,6 @@
     for e in range(1, LINE):
         sums = sums + statr[e - 1]
     zt, zs, lean, pair = (sums[i : i + 1] for i in range(4))
-    part = jnp.sum(lean / zt - jnp.log(zt) + 2.0 * jnp.log(zs) - pair, axis=1, keepdims=True)
-    lossy[...] = jnp.broadcast_to(part, (8, 128))
-    for e in range(1, Y):
-        push(lossy, lossyr.at[e - 1], s_ly.at[e - 1], r_ly.at[e - 1], y_peer(e))
     c_t = jnp.broadcast_to(1.0 / zt, (128, 256)).T
     c_s = jnp.broadcast_to(2.0 / zs, (128, 256)).T
 
@@ -288,6 +271,10 @@
     for e in (3, 5, 4, 1, 7, 2, 6):
         other = rem(q + e, LINE)
         push(dpb.at[rows(other * 32, 32)], rsr.at[e - 1], s_rs.at[e - 1], r_rs.at[e - 1], line_peer(e))
+    part = jnp.sum(lean / zt - jnp.log(zt) + 2.0 * jnp.log(zs) - pair, axis=1, keepdims=True)
+    lossy[...] = jnp.broadcast_to(part, (8, 128))
+    for e in range(1, Y):
+        push(lossy, lossyr.at[e - 1], s_ly.at[e - 1], r_ly.at[e - 1], y_peer(e))
     for e in range(1, Y):
         arrived(lossyr.at[e - 1], r_ly.at[e - 1])
     lossz[...] = lossy[...] + lossyr[0] + lossyr[1] + lossyr[2]
@@ -407,7 +394,7 @@
     scratch = [
         vm((128, 768), BF16), vm((128, 512), BF16), vm((32, 512), BF16),
         vm((768, 128), BF16), vm((128, 512), BF16), vm((1, 128), jnp.int32),
-        vm((8, 2, 32, 512), BF16), vm((8, 2, 3, 16, 512), BF16), vm((8, 3, 2, 16, 512), BF16),
+        vm((8, 4, 2, 32, 512), BF16),
         vm((512, 512), BF16), vm((2, 8, 128), jnp.int32), vm((256, 128), F32),
         vm((128, 512), F32), vm((3, 32, 512), F32), vm((32, 512), F32), vm((32, 128), F32),
         vm((128, 128), F32), vm((128, 128), BF16),
@@ -418,8 +405,8 @@
         vm((128, 512), BF16), vm((768, 128), BF16), vm((7, 16, 512), BF16), vm((7, 96, 128), BF16),
         vm((160, 128), F32), vm((160, 128), BF16), vm((15, 16, 128), BF16),
         vm((160, 128), BF16), vm((7, 160, 128), BF16),
-        dma((6,)), dma((8, 2)), dma((8, 2)), dma((8, 2)), dma((8, 2)), dma((3,)), dma((3,)),
-        dma((9, 3)), dma((9, 3)),
+        dma((6,)), dma((8, 2)), dma((8, 2)), dma((8, 2)), dma((8, 2)),
+        dma((8, 2, 2)), dma((8, 2, 2)),
         dma((3,)), dma((3,)), dma((7,)), dma((7,)), dma((2,)), dma((2,)), dma((7,)), dma((7,)),
         dma((7,)), dma((7,)), dma((3,)), dma((3,)),
         dma((3,)), dma((3,)), dma((15,)), dma((15,)), dma((2, 7)), dma((2, 7)),
@@ -440,7 +427,7 @@
         ),
         scratch_shapes=scratch,
         compiler_params=pltpu.CompilerParams(
-            collective_id=0, has_side_effects=True, vmem_limit_bytes=48 * 1024 * 1024
+            collective_id=0, has_side_effects=True, vmem_limit_bytes=60 * 1024 * 1024
         ),
     )(clip_feats, teacher_audio, teacher_text, w_first, w_second, pairing.reshape(1, 128))
     return loss.reshape(()), grad_first, grad_second

time: 103 us -> 88 us (0.85)
  the two profiles are of different devices: /device:TPU:24 before, /device:TPU:2 now
where the time goes in v2:
time: 88 us; the launch traced here: 87.8 us
  Pallas kernels  82.9 us (94%)
  local copies, waits for them, and re-layouts  2.52 us (3%)
  between operations  2.41 us (3%)
    pallas_call x1, Pallas kernels, body(): pl.pallas_call(kernel, out_shape=(jax.ShapeDtypeStruct((1, 1), F32), jax....  82.9 us
    unnamed x4, local copies, waits for them, and re-layouts  2.52 us

profile of v2, /device:TPU:2, one launch (start us, length us, event | category | flops | bytes accessed | tf_op | source)
XLA Modules:
  0.0 87.8 jit_solution(6507118902171477346)
XLA Ops:
  0.6 82.9 %shard_map.85 = (f32[1,1]{1,0:T(1,128)}, f32[768,128]{1,0:T(8,128)}, f32[128,512]{1,0:T(8,128)}) custom-call(bf16[128,768]{1,0:T(8,128)(2,1)} %clip_h.1, bf16[128,512]{1,0:T(8,128)(2,1)} %ta_h.1, bf16[32,512]{1,0:T(8,128)(2,1)} %tt_h.1, bf16[768,128]{1,0:T(8,128)(2,1)} %w1_h.1, bf16[128,512]{1,0:T(8,128)(2,1)} %w2_h.1, s32[1,128]{1,0:T(1,128)} %bitcast.2), custom_call_target="tpu_custom_call" | custom-call | tf_op jit(solution)/shard_map/pallas_call | solution.py:415
  84.1 0.0 copy-start
  84.1 1.8 %copy.13 = f32[768,128]{1,0:T(8,128)} copy(f32[768,128]{1,0:T(8,128)} %get-tuple-element.13) | data formatting | bytes 786432
  85.9 0.0 copy-done
  85.9 0.7 copy.14
Async XLA Ops:
  84.1 1.8 %copy-start = (f32[128,512]{1,0:T(8,128)S(1)}, f32[128,512]{1,0:T(8,128)}, u32[]{:S(2)}) copy-start(f32[128,512]{1,0:T(8,128)} %get-tuple-element.14) | copy-start | bytes 786436

commit v3 on v2

--- a/solution.py
+++ b/solution.py
@@ -16,7 +16,8 @@
 TEACHER_SCALE = 14.0
 STUDENT_SCALE = 64.0
 EPS = 1e-6
-TILES = 10
+QUAD = 4
+GROUP = Y * XL * QUAD
 
 
 def dot_nt(left, right):
@@ -37,18 +38,18 @@
     clip_h, ta_h, tt_h, w1_h, w2_h, pair_h,
     loss_o, gf_o, gs_o,
     clip_v, ta_v, tt_v, w1_v, w2_v, pair_v,
-    G, stk, prow, pcol, rawp, rawr, st32, nm32, gprime, hid_v,
-    ET, ES, acc, stat, statr, dp, dpb, rsr, drw,
-    lossy, lossyr, lossz, losszr,
-    gsb, gfb, p1s, p1f, own1, T, p2r, R, RR,
+    G, stk, prow, pcol, rawp, rawr, st32, nm32, gprime, hid_t, clip_t,
+    ET, ES, cf, acc, stat, statr, dp, dpb, rsr, drw,
+    lossy, lossz, W, p1a, p1b, zq, R,
     sem_in, sA, rA, sB, rB, sC, rC,
     s_raw, r_raw, s_stud, r_stud, s_tp, r_tp, s_stat, r_stat, s_rs, r_rs, s_dr, r_dr,
-    s_ly, r_ly, s_lz, r_lz, s_p1, r_p1, s_p2, r_p2, s_p3, r_p3, s_p4, r_p4,
+    s_ly, r_ly, s_lz, r_lz, s_p1, r_p1, s_p2, r_p2, s_p3, r_p3,
 ):
     y, z = lax.axis_index("y"), lax.axis_index("z")
     xl, mp = lax.axis_index("xl"), lax.axis_index("mp")
     q = xl * MP + mp
-    j = y * XL + xl
+    zl, zh = lax.rem(z, QUAD), z // QUAD
+    o = (y * XL + xl) * QUAD + zl
     total = 128 * Y * Z * XL
 
     def rem(v, n):
@@ -68,8 +69,9 @@
         return (y, z, xl, rem(mp + e, MP))
 
     def group_peer(e):
-        other = rem(j + e, Y * XL)
-        return (other // XL, z, rem(other, XL), mp)
+        other = rem(o + e, GROUP)
+        at = (other // (XL * QUAD), zh * QUAD + rem(other, QUAD), rem(other // QUAD, XL), mp)
+        return other, at
 
     def remote(src, dst, send, recv, to):
         return pltpu.make_async_remote_copy(
@@ -130,7 +132,6 @@
     pre = jnp.dot(clip_v[...], w1_v[...], preferred_element_type=F32)
     cdf = 0.5 * (1.0 + lax.erf(pre * 0.7071067811865476))
     hid = (pre * cdf).astype(BF16)
-    hid_v[...] = hid
     rawp[...] = jnp.dot(hid, w2_v[...], preferred_element_type=F32)
     for e in (2, 1, 3):
         other = rem(mp + e, MP)
@@ -147,6 +148,7 @@
     push(stk.at[mine], stk.at[mine], s_tp.at[0], r_tp.at[0], other_x)
     push(prow.at[xl], prow.at[xl], s_tp.at[1], r_tp.at[1], other_x)
     gprime[...] = cdf + pre * (0.3989422804014327 * jnp.exp(-0.5 * pre * pre))
+    hid_t[...] = hid.T
 
     def comm(k):
         for d in (0, 1):
@@ -215,6 +217,7 @@
     stk[own] = student.astype(BF16)
     for e in range(1, LINE):
         push(stk.at[own], stk.at[own], s_stud.at[e - 1], r_stud.at[e - 1], line_peer(e))
+    clip_t[...] = clip_v[...].T
     comm(4)
     theirs = rows((1 - xl) * 128, 128)
     arrived(stk.at[theirs], r_tp.at[0])
@@ -251,35 +254,25 @@
 
     for k in range(8):
         hit = hits(k)
-        coef = jnp.concatenate(
-            [
-                (
-                    ES[k, :, h * 128 : (h + 1) * 128] * c_s
-                    - ET[k, :, h * 128 : (h + 1) * 128] * c_t
-                    - hit[h].astype(F32)
-                ).astype(BF16)
-                for h in (0, 1)
-            ],
-            axis=1,
-        )
-        more = jnp.dot(coef, captions(k), preferred_element_type=F32)
-        if k == 0:
-            dp[...] = more
-        else:
-            dp[...] += more
+        for h in (0, 1):
+            half = pl.ds(h * 128, 128)
+            cf[:, k * 256 + h * 128 : k * 256 + (h + 1) * 128] = (
+                ES[k, :, half] * c_s - ET[k, :, half] * c_t - hit[h].astype(F32)
+            ).astype(BF16)
+    dp[...] = jnp.dot(cf[...], G[...].reshape(2048, 512), preferred_element_type=F32)
     dpb[...] = dp[...].astype(BF16)
     for e in (3, 5, 4, 1, 7, 2, 6):
         other = rem(q + e, LINE)
         push(dpb.at[rows(other * 32, 32)], rsr.at[e - 1], s_rs.at[e - 1], r_rs.at[e - 1], line_peer(e))
     part = jnp.sum(lean / zt - jnp.log(zt) + 2.0 * jnp.log(zs) - pair, axis=1, keepdims=True)
-    lossy[...] = jnp.broadcast_to(part, (8, 128))
+    lossy[y] = jnp.broadcast_to(part, (8, 128))
     for e in range(1, Y):
-        push(lossy, lossyr.at[e - 1], s_ly.at[e - 1], r_ly.at[e - 1], y_peer(e))
+        push(lossy.at[y], lossy.at[y], s_ly.at[e - 1], r_ly.at[e - 1], y_peer(e))
     for e in range(1, Y):
-        arrived(lossyr.at[e - 1], r_ly.at[e - 1])
-    lossz[...] = lossy[...] + lossyr[0] + lossyr[1] + lossyr[2]
+        arrived(lossy.at[rem(y - e, Y)], r_ly.at[e - 1])
+    lossz[z] = lossy[0] + lossy[1] + lossy[2] + lossy[3]
     for e in range(1, Z):
-        push(lossz, losszr.at[e - 1], s_lz.at[e - 1], r_lz.at[e - 1], z_peer(e))
+        push(lossz.at[z], lossz.at[z], s_lz.at[e - 1], r_lz.at[e - 1], z_peer(e))
     dstud = dp[rows(q * 32, 32)]
     for e in range(1, LINE):
         arrived(rsr.at[e - 1], r_rs.at[e - 1])
@@ -295,96 +288,104 @@
         arrived(drw.at[rows(rem(mp - e, MP) * 32, 32)], r_dr.at[e - 1])
 
     draw = drw[...]
-    gs = lax.dot_general(
-        hid_v[...], draw, (((0,), (0,)), ((), ())), preferred_element_type=F32
-    )
-    gsb[...] = gs.astype(BF16)
-    group = Y * XL
-    for e in range(1, group):
-        other = rem(j + e, group)
-        push(gsb.at[rows(other * 16, 16)], p1s.at[e - 1], s_p1.at[0, e - 1], r_p1.at[0, e - 1], group_peer(e))
-    gs_o[...] = gs
+    gs = jnp.dot(hid_t[...], draw, preferred_element_type=F32).astype(BF16)
+    for i in range(4):
+        W[pl.ds(i * 128, 128)] = gs[:, i * 128 : (i + 1) * 128]
+
+    def scatter(e, other, at):
+        return remote(W.at[rows(other * 32, 32)], p1a.at[e - 1], s_p1.at[0, e - 1], r_p1.at[0, e - 1], at)
+
+    def scatter_more(e, other, at):
+        return remote(
+            W.at[rows(1024 + other * 16, 16)], p1b.at[e - 1], s_p1.at[1, e - 1], r_p1.at[1, e - 1], at
+        )
+
+    for e in range(1, GROUP):
+        other, at = group_peer(e)
+
+        @pl.when(other < 16)
+        def _():
+            scatter(e, other, at).start()
+
     dpre = (dot_nt(draw, w2_v[...]) * gprime[...]).astype(BF16)
-    gf = lax.dot_general(
-        clip_v[...], dpre, (((0,), (0,)), ((), ())), preferred_element_type=F32
-    )
-    gfb[...] = gf.astype(BF16)
-    for e in range(1, group):
-        other = rem(j + e, group)
-        push(gfb.at[rows(other * 96, 96)], p1f.at[e - 1], s_p1.at[1, e - 1], r_p1.at[1, e - 1], group_peer(e))
-    gf_o[...] = gf
-    one_s = gs_o[rows(j * 16, 16)]
-    one_f = gf_o[rows(j * 96, 96)]
-    for e in range(1, group):
-        arrived(p1s.at[e - 1], r_p1.at[0, e - 1])
-        one_s = one_s + p1s[e - 1].astype(F32)
-    for e in range(1, group):
-        arrived(p1f.at[e - 1], r_p1.at[1, e - 1])
-        one_f = one_f + p1f[e - 1].astype(F32)
-    own1[pl.ds(0, 96)] = one_f
+    W[pl.ds(512, 768)] = jnp.dot(clip_t[...], dpre, preferred_element_type=F32).astype(BF16)
+    for e in range(1, GROUP):
+        other, at = group_peer(e)
+
+        @pl.when(other >= 16)
+        def _():
+            scatter(e, other, at).start()
+
+        @pl.when(other < 16)
+        def _():
+            scatter_more(e, other, at).start()
+
+    part = W[rows(o * 32, 32)].astype(F32)
+    for e in range(1, GROUP):
+        arrived(p1a.at[e - 1], r_p1.at[0, e - 1])
+        part = part + p1a[e - 1].astype(F32)
+    zq[zh, pl.ds(0, 32)] = part.astype(BF16)
+    zq[zh, pl.ds(32, 16)] = jnp.zeros((16, 128), BF16)
+
+    @pl.when(o < 16)
+    def _():
+        more = W[rows(1024 + o * 16, 16)].astype(F32)
+        for e in range(1, GROUP):
+            arrived(p1b.at[e - 1], r_p1.at[1, e - 1])
+            more = more + p1b[e - 1].astype(F32)
+        zq[zh, pl.ds(32, 16)] = more.astype(BF16)
+
+    for e in range(1, QUAD):
+        push(zq.at[zh], zq.at[zh], s_p2.at[e - 1], r_p2.at[e - 1], z_peer(QUAD * e))
+    for e in range(1, Z):
+        arrived(lossz.at[rem(z - e, Z)], r_lz.at[e - 1])
+    loss_sum = lossz[0]
+    for i in range(1, Z):
+        loss_sum = loss_sum + lossz[i]
+    loss_o[0, 0] = jnp.sum(loss_sum[0:1, 0:1]) / total
+    for e in range(1, QUAD):
+        arrived(zq.at[rem(zh - e, QUAD)], r_p2.at[e - 1])
+    whole = zq[0].astype(F32)
+    for i in range(1, QUAD):
+        whole = whole + zq[i].astype(F32)
+    whole = whole.astype(BF16)
+    first, second = rows(o * 32, 32), rows(1024 + o * 16, 16)
+    R[first] = whole[:32]
+    for e in range(1, GROUP):
+        push(R.at[first], R.at[first], s_p3.at[0, e - 1], r_p3.at[0, e - 1], group_peer(e)[1])
+
+    @pl.when(o < 16)
+    def _():
+        R[second] = whole[32:]
+        for e in range(1, GROUP):
+            remote(R.at[second], R.at[second], s_p3.at[1, e - 1], r_p3.at[1, e - 1], group_peer(e)[1]).start()
+
+    for e in range(1, GROUP):
+        other = rem(o - e, GROUP)
+        arrived(R.at[rows(other * 32, 32)], r_p3.at[0, e - 1])
+
+        @pl.when(other < 16)
+        def _():
+            arrived(R.at[rows(1024 + other * 16, 16)], r_p3.at[1, e - 1])
+
     for i in range(4):
-        own1[pl.ds(96 + 16 * i, 16)] = one_s[:, i * 128 : (i + 1) * 128]
-    T[...] = own1[...].astype(BF16)
-    for t in range(TILES):
-
-        @pl.when(z != t)
-        def _():
-            slot = rem(z - t, Z) - 1
-            remote(
-                T.at[pl.ds(16 * t, 16)], p2r.at[slot], s_p2.at[t], r_p2.at[slot], (y, t, xl, mp)
-            ).start()
-
-    loss_sum = lossz[...]
-    for e in range(1, Z):
-        arrived(losszr.at[e - 1], r_lz.at[e - 1])
-        loss_sum = loss_sum + losszr[e - 1]
-    loss_o[0, 0] = jnp.sum(loss_sum[0:1, 0:1]) / total
-
-    @pl.when(z < TILES)
-    def _():
-        tile = rows(z * 16, 16)
-        out = own1[tile]
-        for e in range(1, Z):
-            arrived(p2r.at[e - 1], r_p2.at[e - 1])
-            out = out + p2r[e - 1].astype(F32)
-        R[tile] = out.astype(BF16)
-        for e in range(1, Z):
-            remote(R.at[tile], R.at[tile], s_p3.at[e - 1], r_p3.at[z], z_peer(e)).start()
-
-    for t in range(TILES):
-
-        @pl.when(z != t)
-        def _():
-            arrived(R.at[pl.ds(16 * t, 16)], r_p3.at[t])
-
-    for e in range(1, group):
-        push(R, RR.at[e - 1], s_p4.at[e - 1], r_p4.at[e - 1], group_peer(e))
-
-    def write(owner, ref):
-        gf_o[rows(owner * 96, 96)] = ref[pl.ds(0, 96)].astype(F32)
-        for i in range(4):
-            gs_o[rows(owner * 16, 16), i * 128 : (i + 1) * 128] = ref[
-                pl.ds(96 + 16 * i, 16)
-            ].astype(F32)
-
-    write(j, R)
-    for e in range(1, group):
-        arrived(RR.at[e - 1], r_p4.at[e - 1])
-        write(rem(j - e, group), RR.at[e - 1])
+        gs_o[:, i * 128 : (i + 1) * 128] = R[pl.ds(i * 128, 128)].astype(F32)
+    gf_o[...] = R[pl.ds(512, 768)].astype(F32)
 
     for copy in sends:
         copy.wait_send()
-    for t in range(TILES):
-
-        @pl.when(z != t)
+    for e in range(1, GROUP):
+        other, at = group_peer(e)
+        scatter(e, other, at).wait_send()
+
+        @pl.when(other < 16)
         def _():
-            remote(T.at[pl.ds(16 * t, 16)], T.at[pl.ds(16 * t, 16)], s_p2.at[t], s_p2.at[t], me).wait_send()
-
-    @pl.when(z < TILES)
+            scatter_more(e, other, at).wait_send()
+
+    @pl.when(o < 16)
     def _():
-        tile = rows(z * 16, 16)
-        for e in range(1, Z):
-            remote(R.at[tile], R.at[tile], s_p3.at[e - 1], s_p3.at[e - 1], me).wait_send()
+        for e in range(1, GROUP):
+            remote(R.at[second], R.at[second], s_p3.at[1, e - 1], r_p3.at[1, e - 1], me).wait_send()
 
 
 def body(clip_feats, teacher_audio, teacher_text, w_first, w_second, pairing):
@@ -397,20 +398,19 @@
         vm((8, 4, 2, 32, 512), BF16),
         vm((512, 512), BF16), vm((2, 8, 128), jnp.int32), vm((256, 128), F32),
         vm((128, 512), F32), vm((3, 32, 512), F32), vm((32, 512), F32), vm((32, 128), F32),
-        vm((128, 128), F32), vm((128, 128), BF16),
-        vm((8, 256, 256), F32), vm((8, 256, 256), F32), vm((4, 256, 128), F32),
+        vm((128, 128), F32), vm((128, 128), BF16), vm((768, 128), BF16),
+        vm((8, 256, 256), F32), vm((8, 256, 256), F32), vm((256, 2048), BF16), vm((4, 256, 128), F32),
         vm((8, 256), F32), vm((7, 8, 256), F32),
         vm((256, 512), F32), vm((256, 512), BF16), vm((7, 32, 512), BF16), vm((128, 512), BF16),
-        vm((8, 128), F32), vm((3, 8, 128), F32), vm((8, 128), F32), vm((15, 8, 128), F32),
-        vm((128, 512), BF16), vm((768, 128), BF16), vm((7, 16, 512), BF16), vm((7, 96, 128), BF16),
-        vm((160, 128), F32), vm((160, 128), BF16), vm((15, 16, 128), BF16),
-        vm((160, 128), BF16), vm((7, 160, 128), BF16),
+        vm((Y, 8, 128), F32), vm((Z, 8, 128), F32), vm((1280, 128), BF16),
+        vm((GROUP - 1, 32, 128), BF16), vm((GROUP - 1, 16, 128), BF16), vm((QUAD, 48, 128), BF16),
+        vm((1280, 128), BF16),
         dma((6,)), dma((8, 2)), dma((8, 2)), dma((8, 2)), dma((8, 2)),
         dma((8, 2, 2)), dma((8, 2, 2)),
         dma((3,)), dma((3,)), dma((7,)), dma((7,)), dma((2,)), dma((2,)), dma((7,)), dma((7,)),
         dma((7,)), dma((7,)), dma((3,)), dma((3,)),
-        dma((3,)), dma((3,)), dma((15,)), dma((15,)), dma((2, 7)), dma((2, 7)),
-        dma((TILES,)), dma((15,)), dma((15,)), dma((TILES,)), dma((7,)), dma((7,)),
+        dma((3,)), dma((3,)), dma((15,)), dma((15,)), dma((2, GROUP - 1)), dma((2, GROUP - 1)),
+        dma((QUAD - 1,)), dma((QUAD - 1,)), dma((2, GROUP - 1)), dma((2, GROUP - 1)),
     ]
     loss, grad_first, grad_second = pl.pallas_call(
         kernel,

time: 88 us -> 89.1 us (1.012)
  the two profiles are of different devices: /device:TPU:2 before, /device:TPU:24 now
where the time goes in v3:
time: 89.1 us; the launch traced here: 88.9 us
  Pallas kernels  84 us (94%)
  local copies, waits for them, and re-layouts  2.52 us (3%)
  between operations  2.41 us (3%)
    pallas_call x1, Pallas kernels, body(): pl.pallas_call(kernel, out_shape=(jax.ShapeDtypeStruct((1, 1), F32), jax....  84 us
    unnamed x4, local copies, waits for them, and re-layouts  2.52 us

profile of v3, /device:TPU:24, one launch (start us, length us, event | category | flops | bytes accessed | tf_op | source)
XLA Modules:
  0.0 88.9 jit_solution(9199477504015903899)
XLA Ops:
  0.6 84.0 %shard_map.85 = (f32[1,1]{1,0:T(1,128)}, f32[768,128]{1,0:T(8,128)}, f32[128,512]{1,0:T(8,128)}) custom-call(bf16[128,768]{1,0:T(8,128)(2,1)} %clip_h.1, bf16[128,512]{1,0:T(8,128)(2,1)} %ta_h.1, bf16[32,512]{1,0:T(8,128)(2,1)} %tt_h.1, bf16[768,128]{1,0:T(8,128)(2,1)} %w1_h.1, bf16[128,512]{1,0:T(8,128)(2,1)} %w2_h.1, s32[1,128]{1,0:T(1,128)} %bitcast.2), custom_call_target="tpu_custom_call" | custom-call | tf_op jit(solution)/shard_map/pallas_call | solution.py:415
  85.3 0.0 copy-start
  85.3 1.8 %copy.13 = f32[768,128]{1,0:T(8,128)} copy(f32[768,128]{1,0:T(8,128)} %get-tuple-element.13) | data formatting | bytes 786432
  87.1 0.0 copy-done
  87.1 0.7 copy.14
Async XLA Ops:
  85.3 1.8 %copy-start = (f32[128,512]{1,0:T(8,128)S(1)}, f32[128,512]{1,0:T(8,128)}, u32[]{:S(2)}) copy-start(f32[128,512]{1,0:T(8,128)} %get-tuple-element.14) | copy-start | bytes 786436

commit v4 on v3

--- a/solution.py
+++ b/solution.py
@@ -16,8 +16,9 @@
 TEACHER_SCALE = 14.0
 STUDENT_SCALE = 64.0
 EPS = 1e-6
-QUAD = 4
-GROUP = Y * XL * QUAD
+GROUP = Y * XL
+SLICE = 160
+TILES = 10
 
 
 def dot_nt(left, right):
@@ -36,20 +37,19 @@
 
 def kernel(
     clip_h, ta_h, tt_h, w1_h, w2_h, pair_h,
-    loss_o, gf_o, gs_o,
+    loss_o, gf_h, gs_h,
     clip_v, ta_v, tt_v, w1_v, w2_v, pair_v,
     G, stk, prow, pcol, rawp, rawr, st32, nm32, gprime, hid_t, clip_t,
     ET, ES, cf, acc, stat, statr, dp, dpb, rsr, drw,
-    lossy, lossz, W, p1a, p1b, zq, R,
+    lossy, lossz, W, p1, own1, T, p2r, R, Rs,
     sem_in, sA, rA, sB, rB, sC, rC,
     s_raw, r_raw, s_stud, r_stud, s_tp, r_tp, s_stat, r_stat, s_rs, r_rs, s_dr, r_dr,
-    s_ly, r_ly, s_lz, r_lz, s_p1, r_p1, s_p2, r_p2, s_p3, r_p3,
+    s_ly, r_ly, s_lz, r_lz, s_p1, r_p1, s_p2, r_p2, s_p3, r_p3, s_p4, r_p4,
 ):
     y, z = lax.axis_index("y"), lax.axis_index("z")
     xl, mp = lax.axis_index("xl"), lax.axis_index("mp")
     q = xl * MP + mp
-    zl, zh = lax.rem(z, QUAD), z // QUAD
-    o = (y * XL + xl) * QUAD + zl
+    j = y * XL + xl
     total = 128 * Y * Z * XL
 
     def rem(v, n):
@@ -69,9 +69,8 @@
         return (y, z, xl, rem(mp + e, MP))
 
     def group_peer(e):
-        other = rem(o + e, GROUP)
-        at = (other // (XL * QUAD), zh * QUAD + rem(other, QUAD), rem(other // QUAD, XL), mp)
-        return other, at
+        other = rem(j + e, GROUP)
+        return other, (other // XL, z, rem(other, XL), mp)
 
     def remote(src, dst, send, recv, to):
         return pltpu.make_async_remote_copy(
@@ -217,7 +216,6 @@
     stk[own] = student.astype(BF16)
     for e in range(1, LINE):
         push(stk.at[own], stk.at[own], s_stud.at[e - 1], r_stud.at[e - 1], line_peer(e))
-    clip_t[...] = clip_v[...].T
     comm(4)
     theirs = rows((1 - xl) * 128, 128)
     arrived(stk.at[theirs], r_tp.at[0])
@@ -235,6 +233,8 @@
     for k in (3, 4, 5, 6, 7, 0):
         complete(k)
         chunk(k)
+        if k == 3:
+            clip_t[...] = clip_v[...].T
 
     lane = lax.broadcasted_iota(jnp.int32, (256, 128), 1)
     cols = jnp.zeros((256, 128), F32)
@@ -289,103 +289,96 @@
 
     draw = drw[...]
     gs = jnp.dot(hid_t[...], draw, preferred_element_type=F32).astype(BF16)
-    for i in range(4):
-        W[pl.ds(i * 128, 128)] = gs[:, i * 128 : (i + 1) * 128]
-
-    def scatter(e, other, at):
-        return remote(W.at[rows(other * 32, 32)], p1a.at[e - 1], s_p1.at[0, e - 1], r_p1.at[0, e - 1], at)
-
-    def scatter_more(e, other, at):
-        return remote(
-            W.at[rows(1024 + other * 16, 16)], p1b.at[e - 1], s_p1.at[1, e - 1], r_p1.at[1, e - 1], at
-        )
-
+    for jj in range(GROUP):
+        for i in range(4):
+            W[pl.ds(jj * SLICE + 96 + i * 16, 16)] = gs[jj * 16 : (jj + 1) * 16, i * 128 : (i + 1) * 128]
+
+    def scatter(part, start, size):
+        for e in range(1, GROUP):
+            other, at = group_peer(e)
+            src = W.at[pl.ds(pl.multiple_of(other * SLICE + start, 32), size)]
+            push(src, p1.at[e - 1, pl.ds(start, size)], s_p1.at[part, e - 1], r_p1.at[part, e - 1], at)
+
+    scatter(0, 96, 64)
+    dpre = (dot_nt(draw, w2_v[...]) * gprime[...]).astype(BF16)
+    gf = jnp.dot(clip_t[...], dpre, preferred_element_type=F32).astype(BF16)
+    for jj in range(GROUP):
+        W[pl.ds(jj * SLICE, 96)] = gf[jj * 96 : (jj + 1) * 96]
+    scatter(1, 0, 96)
+    part = W[rows(j * SLICE, SLICE)].astype(F32)
     for e in range(1, GROUP):
-        other, at = group_peer(e)
-
-        @pl.when(other < 16)
+        arrived(p1.at[e - 1, pl.ds(96, 64)], r_p1.at[0, e - 1])
+        arrived(p1.at[e - 1, pl.ds(0, 96)], r_p1.at[1, e - 1])
+        part = part + p1[e - 1].astype(F32)
+    own1[...] = part
+    T[...] = part.astype(BF16)
+
+    def to_owner(t):
+        owner = 8 * t // 5
+        slot = rem(z - owner, Z) - 1
+        tile = T.at[pl.ds(16 * t, 16)]
+        return remote(tile, p2r.at[slot], s_p2.at[t], r_p2.at[slot], (y, owner, xl, mp))
+
+    for t in range(TILES):
+
+        @pl.when(z != 8 * t // 5)
         def _():
-            scatter(e, other, at).start()
-
-    dpre = (dot_nt(draw, w2_v[...]) * gprime[...]).astype(BF16)
-    W[pl.ds(512, 768)] = jnp.dot(clip_t[...], dpre, preferred_element_type=F32).astype(BF16)
-    for e in range(1, GROUP):
-        other, at = group_peer(e)
-
-        @pl.when(other >= 16)
-        def _():
-            scatter(e, other, at).start()
-
-        @pl.when(other < 16)
-        def _():
-            scatter_more(e, other, at).start()
-
-    part = W[rows(o * 32, 32)].astype(F32)
-    for e in range(1, GROUP):
-        arrived(p1a.at[e - 1], r_p1.at[0, e - 1])
-        part = part + p1a[e - 1].astype(F32)
-    zq[zh, pl.ds(0, 32)] = part.astype(BF16)
-    zq[zh, pl.ds(32, 16)] = jnp.zeros((16, 128), BF16)
-
-    @pl.when(o < 16)
+            to_owner(t).start()
+
+    my_tile = lax.min((5 * z + 7) // 8, TILES - 1)
+    owns = 8 * my_tile // 5 == z
+    tile = rows(my_tile * 16, 16)
+
+    @pl.when(owns)
     def _():
-        more = W[rows(1024 + o * 16, 16)].astype(F32)
-        for e in range(1, GROUP):
-            arrived(p1b.at[e - 1], r_p1.at[1, e - 1])
-            more = more + p1b[e - 1].astype(F32)
-        zq[zh, pl.ds(32, 16)] = more.astype(BF16)
-
-    for e in range(1, QUAD):
-        push(zq.at[zh], zq.at[zh], s_p2.at[e - 1], r_p2.at[e - 1], z_peer(QUAD * e))
+        out = own1[tile]
+        for e in range(1, Z):
+            arrived(p2r.at[e - 1], r_p2.at[e - 1])
+            out = out + p2r[e - 1].astype(F32)
+        R[tile] = out.astype(BF16)
+        for e in range(1, Z):
+            remote(R.at[tile], R.at[tile], s_p3.at[e - 1], r_p3.at[my_tile], z_peer(e)).start()
+
     for e in range(1, Z):
         arrived(lossz.at[rem(z - e, Z)], r_lz.at[e - 1])
     loss_sum = lossz[0]
     for i in range(1, Z):
         loss_sum = loss_sum + lossz[i]
     loss_o[0, 0] = jnp.sum(loss_sum[0:1, 0:1]) / total
-    for e in range(1, QUAD):
-        arrived(zq.at[rem(zh - e, QUAD)], r_p2.at[e - 1])
-    whole = zq[0].astype(F32)
-    for i in range(1, QUAD):
-        whole = whole + zq[i].astype(F32)
-    whole = whole.astype(BF16)
-    first, second = rows(o * 32, 32), rows(1024 + o * 16, 16)
-    R[first] = whole[:32]
-    for e in range(1, GROUP):
-        push(R.at[first], R.at[first], s_p3.at[0, e - 1], r_p3.at[0, e - 1], group_peer(e)[1])
-
-    @pl.when(o < 16)
-    def _():
-        R[second] = whole[32:]
+
+    for t in range(TILES):
+
+        @pl.when(z != 8 * t // 5)
+        def _():
+            arrived(R.at[pl.ds(16 * t, 16)], r_p3.at[t])
+
+    Rs[...] = jnp.concatenate([R[pl.ds(96 + i * 16, 16)] for i in range(4)], axis=1)
+    mine = [(R.at[pl.ds(0, 96)], gf_h.at[rows(j * 96, 96)]), (Rs, gs_h.at[rows(j * 16, 16)])]
+    keep = []
+    for i, (src, dst) in enumerate(mine):
         for e in range(1, GROUP):
-            remote(R.at[second], R.at[second], s_p3.at[1, e - 1], r_p3.at[1, e - 1], group_peer(e)[1]).start()
-
-    for e in range(1, GROUP):
-        other = rem(o - e, GROUP)
-        arrived(R.at[rows(other * 32, 32)], r_p3.at[0, e - 1])
-
-        @pl.when(other < 16)
-        def _():
-            arrived(R.at[rows(1024 + other * 16, 16)], r_p3.at[1, e - 1])
-
-    for i in range(4):
-        gs_o[:, i * 128 : (i + 1) * 128] = R[pl.ds(i * 128, 128)].astype(F32)
-    gf_o[...] = R[pl.ds(512, 768)].astype(F32)
-
+            push(src, dst, s_p4.at[i, e - 1], r_p4.at[i, e - 1], group_peer(e)[1])
+        keep.append(pltpu.make_async_copy(src, dst, sem_in.at[6 + i]))
+        keep[-1].start()
     for copy in sends:
         copy.wait_send()
+    for t in range(TILES):
+
+        @pl.when(z != 8 * t // 5)
+        def _():
+            to_owner(t).wait_send()
+
+    @pl.when(owns)
+    def _():
+        for e in range(1, Z):
+            remote(R.at[tile], R.at[tile], s_p3.at[e - 1], s_p3.at[e - 1], me).wait_send()
+
+    for copy in keep:
+        copy.wait()
     for e in range(1, GROUP):
-        other, at = group_peer(e)
-        scatter(e, other, at).wait_send()
-
-        @pl.when(other < 16)
-        def _():
-            scatter_more(e, other, at).wait_send()
-
-    @pl.when(o < 16)
-    def _():
-        for e in range(1, GROUP):
-            remote(R.at[second], R.at[second], s_p3.at[1, e - 1], r_p3.at[1, e - 1], me).wait_send()
+        other = rem(j - e, GROUP)
+        arrived(gf_h.at[rows(other * 96, 96)], r_p4.at[0, e - 1])
+        arrived(gs_h.at[rows(other * 16, 16)], r_p4.at[1, e - 1])
 
 
 def body(clip_feats, teacher_audio, teacher_text, w_first, w_second, pairing):
@@ -403,34 +396,30 @@
         vm((8, 256), F32), vm((7, 8, 256), F32),
         vm((256, 512), F32), vm((256, 512), BF16), vm((7, 32, 512), BF16), vm((128, 512), BF16),
         vm((Y, 8, 128), F32), vm((Z, 8, 128), F32), vm((1280, 128), BF16),
-        vm((GROUP - 1, 32, 128), BF16), vm((GROUP - 1, 16, 128), BF16), vm((QUAD, 48, 128), BF16),
-        vm((1280, 128), BF16),
-        dma((6,)), dma((8, 2)), dma((8, 2)), dma((8, 2)), dma((8, 2)),
+        vm((GROUP - 1, SLICE, 128), BF16), vm((SLICE, 128), F32), vm((SLICE, 128), BF16),
+        vm((Z - 1, 16, 128), BF16), vm((SLICE, 128), BF16), vm((16, 512), BF16),
+        dma((8,)), dma((8, 2)), dma((8, 2)), dma((8, 2)), dma((8, 2)),
         dma((8, 2, 2)), dma((8, 2, 2)),
         dma((3,)), dma((3,)), dma((7,)), dma((7,)), dma((2,)), dma((2,)), dma((7,)), dma((7,)),
         dma((7,)), dma((7,)), dma((3,)), dma((3,)),
         dma((3,)), dma((3,)), dma((15,)), dma((15,)), dma((2, GROUP - 1)), dma((2, GROUP - 1)),
-        dma((QUAD - 1,)), dma((QUAD - 1,)), dma((2, GROUP - 1)), dma((2, GROUP - 1)),
+        dma((TILES,)), dma((Z - 1,)), dma((Z - 1,)), dma((TILES,)), dma((2, GROUP - 1)), dma((2, GROUP - 1)),
     ]
     loss, grad_first, grad_second = pl.pallas_call(
         kernel,
         out_shape=(
             jax.ShapeDtypeStruct((1, 1), F32),
-            jax.ShapeDtypeStruct((768, 128), F32),
-            jax.ShapeDtypeStruct((128, 512), F32),
+            jax.ShapeDtypeStruct((768, 128), BF16),
+            jax.ShapeDtypeStruct((128, 512), BF16),
         ),
         in_specs=[hbm] * 6,
-        out_specs=(
-            pl.BlockSpec(memory_space=pltpu.SMEM),
-            pl.BlockSpec(memory_space=pltpu.VMEM),
-            pl.BlockSpec(memory_space=pltpu.VMEM),
-        ),
+        out_specs=(pl.BlockSpec(memory_space=pltpu.SMEM), hbm, hbm),
         scratch_shapes=scratch,
         compiler_params=pltpu.CompilerParams(
             collective_id=0, has_side_effects=True, vmem_limit_bytes=60 * 1024 * 1024
         ),
     )(clip_feats, teacher_audio, teacher_text, w_first, w_second, pairing.reshape(1, 128))
-    return loss.reshape(()), grad_first, grad_second
+    return loss.reshape(()), grad_first.astype(F32), grad_second.astype(F32)
 
 
 def solution(mesh):

time: 89.1 us -> 86.2 us (0.967)
  Pallas kernels: 84 us -> 80.4 us
  local copies, waits for them, and re-layouts: 2.52 us -> 0.01 us
  other arithmetic: 0 us -> 2.46 us
    pallas_call x1, Pallas kernels: 84 us -> 80.4 us  [body(): pl.pallas_call(kernel, out_shape=(jax.ShapeDtypeStruct((1, 1), F32), jax....]
    unnamed x4 -> x2, local copies, waits for them, and re-layouts: 2.52 us -> 0.01 us
    convert_element_type x0 -> x2, other arithmetic: none -> 2.46 us  [body(): return (loss.reshape(()), grad_first.astype(F32), grad_second.astype(F32))]
where the time goes in v4:
time: 86.2 us; the launch traced here: 85.2 us
  Pallas kernels  80.4 us (93%)
  other arithmetic  2.46 us (3%)
  between operations  2.4 us (3%)
    pallas_call x1, Pallas kernels, body(): pl.pallas_call(kernel, out_shape=(jax.ShapeDtypeStruct((1, 1), F32), jax....  80.4 us
    convert_element_type x2, other arithmetic, body(): return (loss.reshape(()), grad_first.astype(F32), grad_second.astype(F32))  2.46 us

profile of v4, /device:TPU:24, one launch (start us, length us, event | category | flops | bytes accessed | tf_op | source)
XLA Modules:
  0.0 85.2 jit_solution(5921739980194674522)
XLA Ops:
  0.6 80.4 %shard_map.85 = (f32[1,1]{1,0:T(1,128)}, bf16[768,128]{1,0:T(8,128)(2,1)}, bf16[128,512]{1,0:T(8,128)(2,1)}) custom-call(bf16[128,768]{1,0:T(8,128)(2,1)} %clip_h.1, bf16[128,512]{1,0:T(8,128)(2,1)} %ta_h.1, bf16[32,512]{1,0:T(8,128)(2,1)} %tt_h.1, bf16[768,128]{1,0:T(8,128)(2,1)} %w1_h.1, bf16[128,512]{1,0:T(8,128)(2,1)} %w2_h.1, s32[1,128]{1,0:T(1,128)} %bitcast.2), custom_call_target="tpu_custom_call" | custom-call | tf_op jit(solution)/shard_map/pallas_call | solution.py:408
  81.0 0.0 copy-start
  81.0 1.7 %convert_element_type.6 = f32[768,128]{1,0:T(8,128)} convert(bf16[768,128]{1,0:T(8,128)(2,1)} %get-tuple-element.7) | non-fusion elementwise | flops 98304 | bytes 589824 | tf_op jit(solution)/shard_map/convert_element_type | solution.py:422
  82.8 0.0 copy-done
  82.8 0.7 convert_element_type.7
Async XLA Ops:
  81.0 1.7 %copy-start = (bf16[128,512]{1,0:T(8,128)(2,1)S(1)}, bf16[128,512]{1,0:T(8,128)(2,1)}, u32[]{:S(2)}) copy-start(bf16[128,512]{1,0:T(8,128)(2,1)} %get-tuple-element.8) | copy-start | bytes 393220

commit v5 on v4

--- a/solution.py
+++ b/solution.py
@@ -149,17 +149,20 @@
     gprime[...] = cdf + pre * (0.3989422804014327 * jnp.exp(-0.5 * pre * pre))
     hid_t[...] = hid.T
 
-    def comm(k):
+    def own_block(k):
         for d in (0, 1):
             arrived(G.at[k, 0, d], rA.at[k, d])
             along_z(0, k, d, sA, rA)
         for d in (0, 1):
-            arrived(G.at[k, 2, d], rB.at[k, d])
-            along_z(2, k, d, sB, rB)
+            along_y(k, d)
         for d in (0, 1):
             arrived(G.at[k - 1, 0, d], rA.at[k - 1, d])
             along_y(k - 1, d)
-            along_y(k, d)
+
+    def far_block(k):
+        for d in (0, 1):
+            arrived(G.at[k, 2, d], rB.at[k, d])
+            along_z(2, k, d, sB, rB)
 
     def far():
         for k, d in ((7, 0), (7, 1), (0, 1)):
@@ -204,7 +207,8 @@
                 arrived(G.at[k, Y - e, d], rC.at[k, d, e // 2])
 
     acc[...] = jnp.zeros_like(acc)
-    comm(2)
+    own_block(2)
+    far_block(2)
     for e in range(1, MP):
         arrived(rawr.at[e - 1], r_raw.at[e - 1])
     raw = rawp[rows(mp * 32, 32)] + rawr[0] + rawr[1] + rawr[2]
@@ -216,19 +220,21 @@
     stk[own] = student.astype(BF16)
     for e in range(1, LINE):
         push(stk.at[own], stk.at[own], s_stud.at[e - 1], r_stud.at[e - 1], line_peer(e))
-    comm(4)
+    own_block(4)
+    far_block(4)
     theirs = rows((1 - xl) * 128, 128)
     arrived(stk.at[theirs], r_tp.at[0])
     arrived(prow.at[1 - xl], r_tp.at[1])
     for i in range(XL):
         one = jnp.broadcast_to(prow[i][0:1].astype(F32), (128, 128))
         pcol[pl.ds(i * 128, 128)] = one.T
-    comm(6)
+    own_block(6)
     for e in range(1, LINE):
         arrived(stk.at[rows(256 + rem(q - e, LINE) * 32, 32)], r_stud.at[e - 1])
     for k in (1, 2):
         complete(k)
         chunk(k)
+    far_block(6)
     far()
     for k in (3, 4, 5, 6, 7, 0):
         complete(k)
@@ -265,7 +271,7 @@
         other = rem(q + e, LINE)
         push(dpb.at[rows(other * 32, 32)], rsr.at[e - 1], s_rs.at[e - 1], r_rs.at[e - 1], line_peer(e))
     part = jnp.sum(lean / zt - jnp.log(zt) + 2.0 * jnp.log(zs) - pair, axis=1, keepdims=True)
-    lossy[y] = jnp.broadcast_to(part, (8, 128))
+    lossy[y] = jnp.broadcast_to(part, (1, 128))
     for e in range(1, Y):
         push(lossy.at[y], lossy.at[y], s_ly.at[e - 1], r_ly.at[e - 1], y_peer(e))
     for e in range(1, Y):
@@ -305,13 +311,6 @@
     for jj in range(GROUP):
         W[pl.ds(jj * SLICE, 96)] = gf[jj * 96 : (jj + 1) * 96]
     scatter(1, 0, 96)
-    part = W[rows(j * SLICE, SLICE)].astype(F32)
-    for e in range(1, GROUP):
-        arrived(p1.at[e - 1, pl.ds(96, 64)], r_p1.at[0, e - 1])
-        arrived(p1.at[e - 1, pl.ds(0, 96)], r_p1.at[1, e - 1])
-        part = part + p1[e - 1].astype(F32)
-    own1[...] = part
-    T[...] = part.astype(BF16)
 
     def to_owner(t):
         owner = 8 * t // 5
@@ -319,12 +318,21 @@
         tile = T.at[pl.ds(16 * t, 16)]
         return remote(tile, p2r.at[slot], s_p2.at[t], r_p2.at[slot], (y, owner, xl, mp))
 
-    for t in range(TILES):
-
-        @pl.when(z != 8 * t // 5)
-        def _():
-            to_owner(t).start()
-
+    def summed(which, start, size):
+        part = W[pl.ds(pl.multiple_of(j * SLICE + start, 32), size)].astype(F32)
+        for e in range(1, GROUP):
+            arrived(p1.at[e - 1, pl.ds(start, size)], r_p1.at[which, e - 1])
+            part = part + p1[e - 1, start : start + size].astype(F32)
+        own1[pl.ds(start, size)] = part
+        T[pl.ds(start, size)] = part.astype(BF16)
+        for t in range(start // 16, (start + size) // 16):
+
+            @pl.when(z != 8 * t // 5)
+            def _():
+                to_owner(t).start()
+
+    summed(0, 96, 64)
+    summed(1, 0, 96)
     my_tile = lax.min((5 * z + 7) // 8, TILES - 1)
     owns = 8 * my_tile // 5 == z
     tile = rows(my_tile * 16, 16)
@@ -346,20 +354,26 @@
         loss_sum = loss_sum + lossz[i]
     loss_o[0, 0] = jnp.sum(loss_sum[0:1, 0:1]) / total
 
-    for t in range(TILES):
-
-        @pl.when(z != 8 * t // 5)
-        def _():
-            arrived(R.at[pl.ds(16 * t, 16)], r_p3.at[t])
-
-    Rs[...] = jnp.concatenate([R[pl.ds(96 + i * 16, 16)] for i in range(4)], axis=1)
-    mine = [(R.at[pl.ds(0, 96)], gf_h.at[rows(j * 96, 96)]), (Rs, gs_h.at[rows(j * 16, 16)])]
+    def tiles_arrived(first, last):
+        for t in range(first, last):
+
+            @pl.when(z != 8 * t // 5)
+            def _():
+                arrived(R.at[pl.ds(16 * t, 16)], r_p3.at[t])
+
     keep = []
-    for i, (src, dst) in enumerate(mine):
+
+    def give(i, src, dst):
         for e in range(1, GROUP):
             push(src, dst, s_p4.at[i, e - 1], r_p4.at[i, e - 1], group_peer(e)[1])
         keep.append(pltpu.make_async_copy(src, dst, sem_in.at[6 + i]))
         keep[-1].start()
+
+    tiles_arrived(6, TILES)
+    Rs[...] = jnp.concatenate([R[pl.ds(96 + i * 16, 16)] for i in range(4)], axis=1)
+    give(1, Rs, gs_h.at[rows(j * 16, 16)])
+    tiles_arrived(0, 6)
+    give(0, R.at[pl.ds(0, 96)], gf_h.at[rows(j * 96, 96)])
     for copy in sends:
         copy.wait_send()
     for t in range(TILES):
@@ -395,7 +409,7 @@
         vm((8, 256, 256), F32), vm((8, 256, 256), F32), vm((256, 2048), BF16), vm((4, 256, 128), F32),
         vm((8, 256), F32), vm((7, 8, 256), F32),
         vm((256, 512), F32), vm((256, 512), BF16), vm((7, 32, 512), BF16), vm((128, 512), BF16),
-        vm((Y, 8, 128), F32), vm((Z, 8, 128), F32), vm((1280, 128), BF16),
+        vm((Y, 1, 128), F32), vm((Z, 1, 128), F32), vm((1280, 128), BF16),
         vm((GROUP - 1, SLICE, 128), BF16), vm((SLICE, 128), F32), vm((SLICE, 128), BF16),
         vm((Z - 1, 16, 128), BF16), vm((SLICE, 128), BF16), vm((16, 512), BF16),
         dma((8,)), dma((8, 2)), dma((8, 2)), dma((8, 2)), dma((8, 2)),
@@ -419,7 +433,8 @@
             collective_id=0, has_side_effects=True, vmem_limit_bytes=60 * 1024 * 1024
         ),
     )(clip_feats, teacher_audio, teacher_text, w_first, w_second, pairing.reshape(1, 128))
-    return loss.reshape(()), grad_first.astype(F32), grad_second.astype(F32)
+    grad_second, grad_first = lax.optimization_barrier((grad_second.astype(F32), grad_first))
+    return loss.reshape(()), grad_first.astype(F32), grad_second
 
 
 def solution(mesh):

time: 86.2 us -> 85 us (0.986)
  no operation moved by 1% of the time
where the time goes in v5:
time: 85 us; the launch traced here: 84.4 us
  Pallas kernels  79.6 us (94%)
  other arithmetic  2.44 us (3%)
  between operations  2.4 us (3%)
    pallas_call x1, Pallas kernels, body(): pl.pallas_call(kernel, out_shape=(jax.ShapeDtypeStruct((1, 1), F32), jax....  79.6 us

profile of v5, /device:TPU:24, one launch (start us, length us, event | category | flops | bytes accessed | tf_op | source)
XLA Modules:
  0.0 84.4 jit_solution(13717293113456331681)
XLA Ops:
  0.6 79.6 %shard_map.85 = (f32[1,1]{1,0:T(1,128)}, bf16[768,128]{1,0:T(8,128)(2,1)}, bf16[128,512]{1,0:T(8,128)(2,1)}) custom-call(bf16[128,768]{1,0:T(8,128)(2,1)} %clip_h.1, bf16[128,512]{1,0:T(8,128)(2,1)} %ta_h.1, bf16[32,512]{1,0:T(8,128)(2,1)} %tt_h.1, bf16[768,128]{1,0:T(8,128)(2,1)} %w1_h.1, bf16[128,512]{1,0:T(8,128)(2,1)} %w2_h.1, s32[1,128]{1,0:T(1,128)} %bitcast.2), custom_call_target="tpu_custom_call" | custom-call | tf_op jit(solution)/shard_map/pallas_call | solution.py:422
  80.2 0.0 copy-start
  80.2 1.7 %convert_element_type.6 = f32[128,512]{1,0:T(8,128)} convert(bf16[128,512]{1,0:T(8,128)(2,1)} %get-tuple-element.9) | non-fusion elementwise | flops 65536 | bytes 393216 | tf_op jit(solution)/shard_map/convert_element_type | solution.py:436
  81.9 0.0 copy-done
  81.9 0.8 convert_element_type.7
Async XLA Ops:
  80.2 1.7 %copy-start = (bf16[768,128]{1,0:T(8,128)(2,1)S(1)}, bf16[768,128]{1,0:T(8,128)(2,1)}, u32[]{:S(2)}) copy-start(bf16[768,128]{1,0:T(8,128)(2,1)} %get-tuple-element.11) | copy-start | bytes 589828

commit v6 on v5

--- a/solution.py
+++ b/solution.py
@@ -37,11 +37,11 @@
 
 def kernel(
     clip_h, ta_h, tt_h, w1_h, w2_h, pair_h,
-    loss_o, gf_h, gs_h,
+    loss_h, gf_h, gs_h,
     clip_v, ta_v, tt_v, w1_v, w2_v, pair_v,
     G, stk, prow, pcol, rawp, rawr, st32, nm32, gprime, hid_t, clip_t,
     ET, ES, cf, acc, stat, statr, dp, dpb, rsr, drw,
-    lossy, lossz, W, p1, own1, T, p2r, R, Rs,
+    lossy, lossz, W, p1, own1, T, p2r, R, Rs, loss_s,
     sem_in, sA, rA, sB, rB, sC, rC,
     s_raw, r_raw, s_stud, r_stud, s_tp, r_tp, s_stat, r_stat, s_rs, r_rs, s_dr, r_dr,
     s_ly, r_ly, s_lz, r_lz, s_p1, r_p1, s_p2, r_p2, s_p3, r_p3, s_p4, r_p4,
@@ -352,7 +352,9 @@
     loss_sum = lossz[0]
     for i in range(1, Z):
         loss_sum = loss_sum + lossz[i]
-    loss_o[0, 0] = jnp.sum(loss_sum[0:1, 0:1]) / total
+    loss_s[0, 0] = jnp.sum(loss_sum[0:1, 0:1]) / total
+    keep = [pltpu.make_async_copy(loss_s, loss_h, sem_in.at[8])]
+    keep[0].start()
 
     def tiles_arrived(first, last):
         for t in range(first, last):
@@ -360,8 +362,6 @@
             @pl.when(z != 8 * t // 5)
             def _():
                 arrived(R.at[pl.ds(16 * t, 16)], r_p3.at[t])
-
-    keep = []
 
     def give(i, src, dst):
         for e in range(1, GROUP):
@@ -411,8 +411,8 @@
         vm((256, 512), F32), vm((256, 512), BF16), vm((7, 32, 512), BF16), vm((128, 512), BF16),
         vm((Y, 1, 128), F32), vm((Z, 1, 128), F32), vm((1280, 128), BF16),
         vm((GROUP - 1, SLICE, 128), BF16), vm((SLICE, 128), F32), vm((SLICE, 128), BF16),
-        vm((Z - 1, 16, 128), BF16), vm((SLICE, 128), BF16), vm((16, 512), BF16),
-        dma((8,)), dma((8, 2)), dma((8, 2)), dma((8, 2)), dma((8, 2)),
+        vm((Z - 1, 16, 128), BF16), vm((SLICE, 128), BF16), vm((16, 512), BF16), pltpu.SMEM((1, 1), F32),
+        dma((9,)), dma((8, 2)), dma((8, 2)), dma((8, 2)), dma((8, 2)),
         dma((8, 2, 2)), dma((8, 2, 2)),
         dma((3,)), dma((3,)), dma((7,)), dma((7,)), dma((2,)), dma((2,)), dma((7,)), dma((7,)),
         dma((7,)), dma((7,)), dma((3,)), dma((3,)),
@@ -427,12 +427,12 @@
             jax.ShapeDtypeStruct((128, 512), BF16),
         ),
         in_specs=[hbm] * 6,
-        out_specs=(pl.BlockSpec(memory_space=pltpu.SMEM), hbm, hbm),
+        out_specs=(hbm, hbm, hbm),
         scratch_shapes=scratch,
         compiler_params=pltpu.CompilerParams(
-            collective_id=0, has_side_effects=True, vmem_limit_bytes=60 * 1024 * 1024
+            collective_id=0, has_side_effects=True, vmem_limit_bytes=32 * 1024 * 1024
         ),
-    )(clip_feats, teacher_audio, teacher_text, w_first, w_second, pairing.reshape(1, 128))
+    )(*(pltpu.with_memory_space_constraint(a, pltpu.HBM) for a in (clip_feats, teacher_audio, teacher_text, w_first, w_second, pairing.reshape(1, 128))))
     grad_second, grad_first = lax.optimization_barrier((grad_second.astype(F32), grad_first))
     return loss.reshape(()), grad_first.astype(F32), grad_second
 

time: 85 us -> 83.3 us (0.980)
  other arithmetic: 2.44 us -> 1.5 us
    convert_element_type x1, other arithmetic: 1.67 us -> 0.73 us  [body(): grad_second.astype(F32)]
where the time goes in v6:
time: 83.3 us; the launch traced here: 82.8 us
  Pallas kernels  79 us (95%)
  between operations  2.33 us (3%)
  other arithmetic  1.5 us (2%)
    pallas_call x1, Pallas kernels, body(): pl.pallas_call(kernel, out_shape=(jax.ShapeDtypeStruct((1, 1), F32), jax....  79 us

profile of v6, /device:TPU:24, one launch (start us, length us, event | category | flops | bytes accessed | tf_op | source)
XLA Modules:
  0.0 82.8 jit_solution(16884321064260562538)
XLA Ops:
  0.6 79.0 %shard_map.85 = (f32[1,1]{1,0:T(1,128)}, bf16[768,128]{1,0:T(8,128)(2,1)S(1)}, bf16[128,512]{1,0:T(8,128)(2,1)S(1)}) custom-call(bf16[128,768]{1,0:T(8,128)(2,1)} %clip_h.1, bf16[128,512]{1,0:T(8,128)(2,1)} %ta_h.1, bf16[32,512]{1,0:T(8,128)(2,1)} %tt_h.1, bf16[768,128]{1,0:T(8,128)(2,1)} %w1_h.1, bf16[128,512]{1,0:T(8,128)(2,1)} %w2_h.1, s32[1,128]{1,0:T(1,128)} %bitcast.2), custom_call_target="tpu_custom_call" | custom-call | tf_op jit(solution)/shard_map/pallas_call | solution.py:422
  79.6 0.7 convert_element_type.6
  80.3 0.8 convert_element_type.7

commit v7 on v6

--- a/solution.py
+++ b/solution.py
@@ -29,6 +29,10 @@
 
 def normalize(values):
     return values / jnp.sqrt(jnp.sum(values * values, axis=1, keepdims=True) + EPS)
+
+
+def far_first(size):
+    return sorted(range(1, size), key=lambda e: -min(e, size - e))
 
 
 def rows(start, size):
@@ -300,7 +304,7 @@
             W[pl.ds(jj * SLICE + 96 + i * 16, 16)] = gs[jj * 16 : (jj + 1) * 16, i * 128 : (i + 1) * 128]
 
     def scatter(part, start, size):
-        for e in range(1, GROUP):
+        for e in far_first(GROUP):
             other, at = group_peer(e)
             src = W.at[pl.ds(pl.multiple_of(other * SLICE + start, 32), size)]
             push(src, p1.at[e - 1, pl.ds(start, size)], s_p1.at[part, e - 1], r_p1.at[part, e - 1], at)
@@ -344,7 +348,7 @@
             arrived(p2r.at[e - 1], r_p2.at[e - 1])
             out = out + p2r[e - 1].astype(F32)
         R[tile] = out.astype(BF16)
-        for e in range(1, Z):
+        for e in far_first(Z):
             remote(R.at[tile], R.at[tile], s_p3.at[e - 1], r_p3.at[my_tile], z_peer(e)).start()
 
     for e in range(1, Z):
@@ -364,7 +368,7 @@
                 arrived(R.at[pl.ds(16 * t, 16)], r_p3.at[t])
 
     def give(i, src, dst):
-        for e in range(1, GROUP):
+        for e in far_first(GROUP):
             push(src, dst, s_p4.at[i, e - 1], r_p4.at[i, e - 1], group_peer(e)[1])
         keep.append(pltpu.make_async_copy(src, dst, sem_in.at[6 + i]))
         keep[-1].start()

time: 83.3 us -> 82.8 us (level)
  Pallas kernels: 79 us -> 77.7 us
    pallas_call x1, Pallas kernels: 79 us -> 77.7 us  [body(): pl.pallas_call(kernel, out_shape=(jax.ShapeDtypeStruct((1, 1), F32), jax....]
where the time goes in v7:
time: 82.8 us; the launch traced here: 81.5 us
  Pallas kernels  77.7 us (94%)
  between operations  2.33 us (3%)
  other arithmetic  1.5 us (2%)
    pallas_call x1, Pallas kernels, body(): pl.pallas_call(kernel, out_shape=(jax.ShapeDtypeStruct((1, 1), F32), jax....  77.7 us

profile of v7, /device:TPU:24, one launch (start us, length us, event | category | flops | bytes accessed | tf_op | source)
XLA Modules:
  0.0 81.5 jit_solution(13900282222894426354)
XLA Ops:
  0.6 77.7 %shard_map.85 = (f32[1,1]{1,0:T(1,128)}, bf16[768,128]{1,0:T(8,128)(2,1)S(1)}, bf16[128,512]{1,0:T(8,128)(2,1)S(1)}) custom-call(bf16[128,768]{1,0:T(8,128)(2,1)} %clip_h.1, bf16[128,512]{1,0:T(8,128)(2,1)} %ta_h.1, bf16[32,512]{1,0:T(8,128)(2,1)} %tt_h.1, bf16[768,128]{1,0:T(8,128)(2,1)} %w1_h.1, bf16[128,512]{1,0:T(8,128)(2,1)} %w2_h.1, s32[1,128]{1,0:T(1,128)} %bitcast.2), custom_call_target="tpu_custom_call" | custom-call | tf_op jit(solution)/shard_map/pallas_call | solution.py:426
  78.3 0.7 convert_element_type.6
  79.0 0.8 convert_element_type.7
